TPU v7x, 32 devices: a whole 2x2x4 slice. The times are simulated.
32 devices in a mesh: role: 2 (over y), dp: 16 (over z, x, core).
Axes of the slice: x: 2, y: 2, z: 4, core: 2. Of those that a mesh axis runs over, the one named last changes fastest.
Arguments:
- frames: bfloat16 [2, 128, 121, 2048], P('role', 'dp'), may hold values from -6 to 6
- game_ids: int32 [128], P('dp'), may hold values from 0 to 39, as said below
- taken_actions: int32 [128], P('dp'), may hold values from 0 to 17
- next_actions: int32 [128], P('dp'), may hold values from 0 to 17
- expert_flags: int32 [128], P('dp'), may hold values 0 or 1
- rewards: float32 [128], P('dp'), may hold values from -1 to 1
- done_flags: int32 [128], P('dp'), may hold values 0 or 1
- weight_in: float32 [1, 2048, 512], P(None, 'dp'), may hold values from -0.125 to 0.125
- weight_mid: float32 [1, 4608, 512], P(None, 'dp'), may hold values from -0.09375 to 0.09375
- weight_out: float32 [1, 512, 2048], P(None, 'dp'), may hold values from -0.25 to 0.25
- norm_gains: float32 [1, 6144], P(None, 'dp'), may hold values from 0.5 to 1.5
- head_table: float32 [2048, 36720], P('dp'), may hold values from -0.125 to 0.125
- moment_in: float32 [1, 2048, 512], P(None, 'dp'), may hold values from -0.046875 to 0.046875
- moment_mid: float32 [1, 4608, 512], P(None, 'dp'), may hold values from -0.046875 to 0.046875
- moment_out: float32 [1, 512, 2048], P(None, 'dp'), may hold values from -0.046875 to 0.046875
- moment_gains: float32 [1, 6144], P(None, 'dp'), may hold values from -0.15625 to 0.15625
- moment_head: float32 [2048, 36720], P('dp'), may hold values from -0.046875 to 0.046875
- average_in: float32 [1, 2048, 512], P(None, 'dp'), may hold values from -0.125 to 0.125
- average_mid: float32 [1, 4608, 512], P(None, 'dp'), may hold values from -0.09375 to 0.09375
- average_out: float32 [1, 512, 2048], P(None, 'dp'), may hold values from -0.25 to 0.25
- average_gains: float32 [1, 6144], P(None, 'dp'), may hold values from 0.5 to 1.5
- average_head: float32 [2048, 36720], P('dp'), may hold values from -0.125 to 0.125
Outputs:
- loss_total: float32 [], replicated
- new_weight_in: float32 [1, 2048, 512], P(None, 'dp', 'role')
- gradient_in: float32 [1, 2048, 512], P(None, 'dp', 'role')
- new_average_in: float32 [1, 2048, 512], P(None, 'dp', 'role')
- copy_weight_in: bfloat16 [1, 2048, 512], P(None, 'dp', 'role')
- new_weight_mid: float32 [1, 4608, 512], P(None, 'dp', 'role')
- new_moment_mid: float32 [1, 4608, 512], P(None, 'dp', 'role')
- new_average_mid: float32 [1, 4608, 512], P(None, 'dp', 'role')
- copy_weight_mid: bfloat16 [1, 4608, 512], P(None, 'dp', 'role')
- new_weight_out: float32 [1, 512, 2048], P(None, 'dp', 'role')
- new_moment_out: float32 [1, 512, 2048], P(None, 'dp', 'role')
- new_average_out: float32 [1, 512, 2048], P(None, 'dp', 'role')
- copy_weight_out: bfloat16 [1, 512, 2048], P(None, 'dp', 'role')
- new_norm_gains: float32 [1, 6144], P(None, 'dp')
- new_moment_gains: float32 [1, 6144], P(None, 'dp')
- new_average_gains: float32 [1, 6144], P(None, 'dp')
- copy_norm_gains: bfloat16 [1, 6144], P(None, 'dp')
- new_head_table: float32 [2048, 36720], P('dp', 'role')
- new_moment_head: float32 [2048, 36720], P('dp', 'role')
- new_average_head: float32 [2048, 36720], P('dp', 'role')
- copy_head_table: bfloat16 [2048, 36720], P('dp', 'role')
Inputs may be any that keep to these rules, and one draw needn't show every extreme that they name: `game_ids`: 10 of the games, never game 0 nor game 40 - 1, are never drawn; which ones is drawn from the seed; the other games are equally likely.
All inputs are finite; a program needn't handle non-finite values. No bound on the sum of `expert_flags` or of `done_flags` on one device may be relied on, other than what follows from the above.
Results may differ from a plain program's by a relative error of at most 0.015.
Values may be sent and summed in bfloat16 or wider, within the bound.
A program may use at most 320 MiB of HBM per device.

v0:
```python
import jax
import jax.numpy as jnp
from jax import lax
from jax.sharding import PartitionSpec as P

D = 2048
MID = 512
GAMES = 40
ACTIONS = 18
ATOMS = 51
GROUPS = 32
SIDE = 11
LAYERS = 1


support_low = -10.0
support_high = 10.0
discount = 0.99
penalty = 0.05
momentum_decay = 0.5
average_decay = 0.5
learn_rate = 4.0
gain_rate = 40.0
epsilon = 1e-05
HIGHEST = lax.Precision.HIGHEST


def passed_along(block, axis, distance):
    devices = range(lax.axis_size(axis))
    route = [(i - distance, i) for i in devices if i - distance in devices]
    return lax.ppermute(block, axis, route)


def split_gains(gains):
    return (
        gains[:MID],
        gains[MID : 2 * MID],
        gains[2 * MID : 3 * MID],
        gains[3 * MID : 4 * MID],
        gains[4 * MID : 4 * MID + D],
        gains[4 * MID + D :],
    )


def group_norm(values, gain, shift):
    rows, pixels, width = values.shape
    grouped = values.reshape(rows, pixels, GROUPS, width // GROUPS)
    center = grouped - jnp.mean(grouped, axis=(1, 3), keepdims=True)
    spread = jnp.mean(center * center, axis=(1, 3), keepdims=True)
    normed = (center * lax.rsqrt(spread + epsilon)).reshape(values.shape)
    return normed * gain + shift


def patches_of(acts):
    rows, pixels, width = acts.shape
    grid = acts.reshape(rows, SIDE, SIDE, width)
    padded = jnp.pad(grid, ((0, 0), (1, 1), (1, 1), (0, 0)))
    pieces = [
        padded[:, down : down + SIDE, right : right + SIDE, :]
        for down in range(3)
        for right in range(3)
    ]
    return jnp.concatenate(pieces, axis=-1).reshape(rows, pixels, 9 * width)


def transition_loss(logits, target_dist, action_hot, expert, support):
    log_prob = jax.nn.log_softmax(logits, axis=-1)
    values = jnp.sum(jnp.exp(log_prob) * support, axis=-1)
    spread_sum = jax.nn.logsumexp(values, axis=-1)
    chosen_log = jnp.sum(log_prob * action_hot[:, :, None], axis=1)
    cross = -jnp.sum(target_dist * chosen_log, axis=-1)
    regular = spread_sum - jnp.sum(values * action_hot, axis=-1)
    return cross + penalty * expert * regular


def project_target(next_prob, rewards, done_f, support):
    moved = jnp.clip(
        rewards[:, None] + discount * (1.0 - done_f)[:, None] * support[None, :],
        support_low,
        support_high,
    )
    spacing = (support_high - support_low) / (ATOMS - 1)
    weight = jnp.maximum(0.0, 1.0 - jnp.abs(moved[:, :, None] - support[None, None, :]) / spacing)
    return jnp.sum(next_prob[:, :, None] * weight, axis=1)


def renew(weight, grad, moment, average, rate):
    new_moment = momentum_decay * moment + grad
    new_weight = weight - rate * (grad + momentum_decay * new_moment)
    new_average = average_decay * average + (1.0 - average_decay) * new_weight
    return (new_weight, new_moment, new_average, new_weight.astype(jnp.bfloat16))


def lower_half(values):
    return values[..., : values.shape[-1] // 2]


def upper_half(values):
    return values[..., values.shape[-1] // 2 :]


def own_half(values, role_index):
    half = values.shape[-1] // 2
    return lax.dynamic_slice_in_dim(values, role_index * half, half, values.ndim - 1)


def norm_act(hidden, gain, shift):
    return jax.nn.gelu(group_norm(hidden, gain, shift))


def outer_act(hidden, gain, shift, stream):
    return jax.nn.gelu(stream + group_norm(hidden, gain, shift))


def block_forward(stream, weights):
    w_in, w_mid, w_out, gains = weights
    gain_one, shift_one, gain_two, shift_two, gain_three, shift_three = split_gains(gains)
    stream_low = stream.astype(jnp.bfloat16)
    hidden_in = jnp.einsum("bpc,cm->bpm", stream_low, w_in, preferred_element_type=jnp.float32)
    act_in = norm_act(hidden_in, gain_one, shift_one).astype(jnp.bfloat16)
    hidden_mid = jnp.einsum(
        "bpc,cm->bpm", patches_of(act_in), w_mid, preferred_element_type=jnp.float32
    )
    act_mid = norm_act(hidden_mid, gain_two, shift_two).astype(jnp.bfloat16)
    hidden_out = jnp.einsum("bpc,cm->bpm", act_mid, w_out, preferred_element_type=jnp.float32)
    result = outer_act(hidden_out, gain_three, shift_three, stream)
    return (result, (stream, stream_low, hidden_in, act_in, hidden_mid, act_mid, hidden_out))


def block_backward(grad_result, weights, kept, settle):
    w_in, w_mid, w_out, gains = weights
    stream, stream_low, hidden_in, act_in, hidden_mid, act_mid, hidden_out = kept
    gain_one, shift_one, gain_two, shift_two, gain_three, shift_three = split_gains(gains)
    _, back_three = jax.vjp(outer_act, hidden_out, gain_three, shift_three, stream)
    d_three, dg_three, db_three, d_resid = back_three(grad_result)
    d_three = d_three.astype(jnp.bfloat16)
    grad_out = settle(
        jnp.einsum("bpm,bpc->mc", act_mid, d_three, preferred_element_type=jnp.float32)
    )
    d_act_mid = jnp.einsum("bpc,mc->bpm", d_three, w_out, preferred_element_type=jnp.float32)
    _, back_two = jax.vjp(norm_act, hidden_mid, gain_two, shift_two)
    d_two, dg_two, db_two = back_two(d_act_mid)
    d_two = d_two.astype(jnp.bfloat16)
    grad_mid = settle(
        jnp.einsum("bpk,bpm->km", patches_of(act_in), d_two, preferred_element_type=jnp.float32)
    )
    d_cols = jnp.einsum("bpm,km->bpk", d_two, w_mid, preferred_element_type=jnp.float32)
    _, back_cols = jax.vjp(patches_of, act_in.astype(jnp.float32))
    (d_act_in,) = back_cols(d_cols)
    _, back_one = jax.vjp(norm_act, hidden_in, gain_one, shift_one)
    d_one, dg_one, db_one = back_one(d_act_in)
    d_one = d_one.astype(jnp.bfloat16)
    grad_in = jnp.einsum("bpc,bpm->cm", stream_low, d_one, preferred_element_type=jnp.float32)
    d_stream = d_resid + jnp.einsum("bpm,cm->bpc", d_one, w_in, preferred_element_type=jnp.float32)
    grad_gains = jnp.concatenate([dg_one, db_one, dg_two, db_two, dg_three, db_three])
    grad_in, grad_gains = settle((grad_in, grad_gains))
    return (d_stream, (grad_in, grad_mid, grad_out, grad_gains))


def on_device(
    frames,
    game_ids,
    taken_actions,
    next_actions,
    expert_flags,
    rewards,
    done_flags,
    weight_in,
    weight_mid,
    weight_out,
    norm_gains,
    head_table,
    moment_in,
    moment_mid,
    moment_out,
    moment_gains,
    moment_head,
    average_in,
    average_mid,
    average_out,
    average_gains,
    average_head,
):
    role_index = lax.axis_index("role")
    online = role_index == 0
    use_in = jnp.where(online, weight_in, average_in).astype(jnp.bfloat16)
    use_mid = jnp.where(online, weight_mid, average_mid).astype(jnp.bfloat16)
    use_out = jnp.where(online, weight_out, average_out).astype(jnp.bfloat16)
    use_gains = jnp.where(online, norm_gains, average_gains).astype(jnp.bfloat16)
    use_head = jnp.where(online, head_table, average_head).astype(jnp.bfloat16)
    support = support_low + (support_high - support_low) * jnp.arange(ATOMS, dtype=jnp.float32) / (
        ATOMS - 1
    )
    own_hot = (game_ids[:, None] == lax.broadcasted_iota(jnp.int32, (1, GAMES), 1)).astype(
        jnp.float32
    )
    counts = jnp.sum(own_hot, axis=0)
    stream = frames[0].astype(jnp.float32)
    layer = 0
    pieces = (
        lax.all_gather(use_in[layer], "dp", axis=0, tiled=True),
        lax.all_gather(use_mid[layer], "dp", axis=0, tiled=True),
        lax.all_gather(use_out[layer], "dp", axis=0, tiled=True),
        lax.all_gather(use_gains[layer], "dp", axis=0, tiled=True),
    )
    weights = (pieces[0], pieces[1], pieces[2], pieces[3].astype(jnp.float32))
    stream, saved = block_forward(stream, weights)
    gathered = [weights]
    kept = [saved]
    trans = stream.shape[0]
    pixels = stream.shape[1]
    wide_k = ACTIONS * ATOMS
    head_rows = head_table.shape[0]
    feat_low = jnp.mean(stream, axis=1).astype(jnp.bfloat16)
    feat_all, game_all = (
        lax.all_gather(feat_low, "dp", axis=0, tiled=True),
        lax.all_gather(game_ids.astype(jnp.bfloat16)[:, None], "dp", axis=0, tiled=True),
    )
    game_iota = lax.broadcasted_iota(jnp.int32, (1, GAMES), 1).astype(jnp.float32)
    all_hot = (game_all.astype(jnp.float32) == game_iota).astype(jnp.bfloat16)
    feat_rows = lax.dynamic_slice_in_dim(feat_all, lax.axis_index("dp") * head_rows, head_rows, 1)
    head_low = use_head.reshape(head_rows * GAMES, wide_k)

    def widen(count):
        spread_rows = (feat_rows[:, :, None] * all_hot[:, None, :]).reshape(
            count, head_rows * GAMES
        )
        return (spread_rows, all_hot)

    spread_rows, hot_piece = widen(trans * lax.axis_size("dp"))
    flat_logits = lax.psum_scatter(
        jnp.dot(spread_rows, head_low, preferred_element_type=jnp.float32),
        "dp",
        scatter_dimension=0,
        tiled=True,
    )
    logits = flat_logits.reshape(trans, ACTIONS, ATOMS)
    next_hot = (next_actions[:, None] == lax.broadcasted_iota(jnp.int32, (1, ACTIONS), 1)).astype(
        jnp.float32
    )
    next_prob = jax.nn.softmax(jnp.sum(logits * next_hot[:, :, None], axis=1), axis=-1)
    projected = project_target(next_prob, rewards, done_flags.astype(jnp.float32), support)
    target_dist = passed_along(projected, "role", -1)
    action_hot = (
        taken_actions[:, None] == lax.broadcasted_iota(jnp.int32, (1, ACTIONS), 1)
    ).astype(jnp.float32)
    expert = expert_flags.astype(jnp.float32)

    def local_loss(values):
        return transition_loss(values, target_dist, action_hot, expert, support)

    row_loss, loss_back = jax.vjp(local_loss, logits)
    sums = jnp.dot(row_loss, own_hot, precision=HIGHEST)
    total_counts, total_sums = lax.psum((counts, sums), "dp")
    floor_counts = jnp.maximum(total_counts, 1.0)
    loss_total = jnp.sum(total_sums / floor_counts)
    row_weight = jnp.dot(own_hot, 1.0 / (GAMES * floor_counts), precision=HIGHEST)
    (d_logits,) = loss_back(row_weight)
    d_low = d_logits.reshape(trans, wide_k).astype(jnp.bfloat16)
    piece = lax.all_gather(d_low, "dp", axis=0, tiled=True)
    count = piece.shape[0]
    spread_rows, hot_piece = widen(count)
    grad_head = lax.dot_general(
        spread_rows, piece, (((0,), (0,)), ((), ())), preferred_element_type=jnp.float32
    )
    back_wide = jnp.dot(piece, head_low.T, preferred_element_type=jnp.float32)
    back_rows = jnp.sum(
        back_wide.reshape(count, head_rows, GAMES) * hot_piece[:, None, :].astype(jnp.float32),
        axis=2,
    )
    grad_rows = back_rows
    grad_head, grad_rows = (grad_head, grad_rows)
    feat_grad = lax.all_to_all(
        grad_rows.astype(jnp.bfloat16), "dp", split_axis=0, concat_axis=1, tiled=True
    ).astype(grad_rows.dtype)
    d_stream = jnp.broadcast_to(feat_grad[:, None, :] / pixels, stream.shape)

    def settle(values):
        return values

    layer_grads = [None] * LAYERS
    for layer in reversed(range(LAYERS)):
        d_stream, block_grad = block_backward(d_stream, gathered[layer], kept[layer], settle)
        layer_grads[layer] = block_grad
    stacked = tuple((jnp.stack([layer_grads[0][kind]]) for kind in range(4)))
    reduced = lax.psum_scatter(stacked, "dp", scatter_dimension=1, tiled=True)
    head_grad = grad_head.reshape(head_rows, GAMES * wide_k)
    sent = (
        passed_along(upper_half(reduced[0]).astype(jnp.bfloat16), "role", 1).astype(jnp.float32),
        passed_along(upper_half(reduced[1]).astype(jnp.bfloat16), "role", 1).astype(jnp.float32),
        passed_along(upper_half(reduced[2]).astype(jnp.bfloat16), "role", 1).astype(jnp.float32),
        passed_along(reduced[3].astype(jnp.bfloat16), "role", 1).astype(jnp.float32),
        passed_along(upper_half(head_grad).astype(jnp.bfloat16), "role", 1).astype(jnp.float32),
        passed_along(loss_total.astype(jnp.bfloat16), "role", 1).astype(loss_total.dtype),
    )
    grad_in = jnp.where(online, lower_half(reduced[0]), sent[0])
    grad_mid = jnp.where(online, lower_half(reduced[1]), sent[1])
    grad_out = jnp.where(online, lower_half(reduced[2]), sent[2])
    grad_gains = jnp.where(online, reduced[3], sent[3])
    grad_table = jnp.where(online, lower_half(head_grad), sent[4])
    loss_out = jnp.where(online, loss_total, sent[5])
    in_w, in_m, in_a, in_c = renew(
        own_half(weight_in, role_index),
        grad_in,
        own_half(moment_in, role_index),
        own_half(average_in, role_index),
        learn_rate,
    )
    mid_w, mid_m, mid_a, mid_c = renew(
        own_half(weight_mid, role_index),
        grad_mid,
        own_half(moment_mid, role_index),
        own_half(average_mid, role_index),
        learn_rate,
    )
    out_w, out_m, out_a, out_c = renew(
        own_half(weight_out, role_index),
        grad_out,
        own_half(moment_out, role_index),
        own_half(average_out, role_index),
        learn_rate,
    )
    gain_w, gain_m, gain_a, gain_c = renew(
        norm_gains, grad_gains, moment_gains, average_gains, gain_rate
    )
    head_w, head_m, head_a, head_c = renew(
        own_half(head_table, role_index),
        grad_table,
        own_half(moment_head, role_index),
        own_half(average_head, role_index),
        learn_rate,
    )
    return (
        loss_out,
        in_w,
        grad_in,
        in_a,
        in_c,
        mid_w,
        mid_m,
        mid_a,
        mid_c,
        out_w,
        out_m,
        out_a,
        out_c,
        gain_w,
        gain_m,
        gain_a,
        gain_c,
        head_w,
        head_m,
        head_a,
        head_c,
    )


def solution(mesh):
    return jax.shard_map(
        on_device,
        mesh=mesh,
        in_specs=(
            P("role", "dp", None, None),
            P("dp"),
            P("dp"),
            P("dp"),
            P("dp"),
            P("dp"),
            P("dp"),
            P(None, "dp", None),
            P(None, "dp", None),
            P(None, "dp", None),
            P(None, "dp"),
            P("dp", None),
            P(None, "dp", None),
            P(None, "dp", None),
            P(None, "dp", None),
            P(None, "dp"),
            P("dp", None),
            P(None, "dp", None),
            P(None, "dp", None),
            P(None, "dp", None),
            P(None, "dp"),
            P("dp", None),
        ),
        out_specs=(
            P(),
            P(None, "dp", "role"),
            P(None, "dp", "role"),
            P(None, "dp", "role"),
            P(None, "dp", "role"),
            P(None, "dp", "role"),
            P(None, "dp", "role"),
            P(None, "dp", "role"),
            P(None, "dp", "role"),
            P(None, "dp", "role"),
            P(None, "dp", "role"),
            P(None, "dp", "role"),
            P(None, "dp", "role"),
            P(None, "dp"),
            P(None, "dp"),
            P(None, "dp"),
            P(None, "dp"),
            P("dp", "role"),
            P("dp", "role"),
            P("dp", "role"),
            P("dp", "role"),
        ),
        check_vma=False,
    )
```

profile of v0, /device:TPU:6, one launch (start us, length us, event | category | flops | bytes accessed | tf_op | source)
XLA Modules:
  0.0 829.0 jit_solution(6457589474198371482)
XLA Ops:
  12.7 11.7 %select_convert_fusion = bf16[128,36720]{0,1:T(8,128)(2,1)} fusion(f32[128,36720]{0,1:T(8,128)} %param.33, f32[128,36720]{0,1:T(8,128)} %param.43, pred[]{:T(512)S(6)} %eq.74), kind=kLoop, calls=%fused_computation | loop fusion | flops 4700160 | bytes 47001600 | tf_op jit(solution)/shard_map/convert_element_type | solution.py:190
  24.3 12.7 %copy.310 = bf16[128,36720]{1,0:T(8,128)(2,1)} copy(bf16[128,36720]{0,1:T(8,128)(2,1)} %select_convert_fusion) | data formatting | bytes 18800640 | tf_op jit(solution)/shard_map/convert_element_type | solution.py:190
  37.0 11.3 %dot_general.64 = bf16[128,40,918]{0,2,1:T(8,128)(2,1)} reshape(bf16[128,36720]{0,1:T(8,128)(2,1)} %select_convert_fusion) | data formatting | bytes 18800640 | tf_op jit(solution)/shard_map/dot_general | solution.py:266
  49.9 29.1 %all-reduce.10 = bf16[128]{0:T(256)(128)(2,1)S(1)} all-reduce(bf16[128]{0:T(256)(128)(2,1)S(1)} %dynamic-update-slice), channel_id=6, replica_groups=mesh['role'=2,'dp'=16] {'dp'}, use_global_device_ids=true, to_apply=%add.10 | all-reduce | flops 128 | bytes 512
  79.0 22.3 %all-gather.1 = bf16[1,6144]{1,0:T(2,128)(2,1)S(1)} all-gather(bf16[1,384]{1,0:T(2,128)(2,1)S(1)} %fusion.72), channel_id=3, replica_groups=mesh['role'=2,'dp'=16] {'dp'}, dimensions={1}, use_global_device_ids=true | all-gather | bytes 13056 | tf_op jit(solution)/shard_map/all_gather | solution.py:204
  101.6 21.6 %reshape.524 = bf16[5120,918]{1,0:T(8,128)(2,1)} reshape(bf16[128,36720]{1,0:T(8,128)(2,1)} %copy.310) | data formatting | bytes 18800640 | tf_op jit(solution)/shard_map/reshape | solution.py:222
  165.2 11.0 %fusion.104 = (f32[8,32]{1,0:T(8,128)S(1)}, f32[8,121,32,16]{1,2,3,0:T(8,128)S(1)}) fusion(bf16[32,16,4608]{2,1,0:T(8,128)(2,1)} %bitcast.173, bf16[8,121,4608]{2,1,0:T(8,128)(2,1)} %copy_dynamic-update-slice_fusion), kind=kOutput, calls=%fused_computation.254 | convolution fusion | flops 4568092672 | bytes 15623168 | tf_op jit(solution)/shard_map/bpc,cm->bpm/dot_general | solution.py:121
  206.0 18.4 %all_gather.25 = bf16[128,2048]{1,0:T(8,128)(2,1)S(1)} all-gather(bf16[8,2048]{1,0:T(8,128)(2,1)S(1)} %multiply_convert_fusion.1), channel_id=1, replica_groups=mesh['role'=2,'dp'=16] {'dp'}, dimensions={0}, use_global_device_ids=true | all-gather | bytes 557056 | tf_op jit(solution)/shard_map/all_gather | solution.py:216
  232.5 27.2 %psum.15 = f32[40]{0:T(128)S(1)} all-reduce(f32[40]{0:T(128)S(1)} %convert_reduce_fusion), channel_id=1, replica_groups=mesh['role'=2,'dp'=16] {'dp'}, use_global_device_ids=true, to_apply=%region_24.25 | all-reduce | flops 40 | bytes 320 | tf_op jit(solution)/shard_map/psum | solution.py:254
  259.8 27.2 %reduce-scatter.8.cloned.1.call-done = f32[8,918]{1,0:T(8,128)} async-done(((f32[128,918]{1,0:T(8,128)}), f32[8,918]{1,0:T(8,128)}) %reduce-scatter.8.cloned.1.call-update) | async-done | bytes 29392 | tf_op jit(solution)/shard_map/reduce_scatter | solution.py:231
  295.6 18.4 %all_gather.27 = bf16[128,918]{1,0:T(8,128)(2,1)S(1)} all-gather(bf16[8,918]{1,0:T(8,128)(2,1)S(1)} %add_convert_fusion.4), channel_id=1, replica_groups=mesh['role'=2,'dp'=16] {'dp'}, dimensions={0}, use_global_device_ids=true | all-gather | bytes 249696 | tf_op jit(solution)/shard_map/all_gather | solution.py:260
  334.0 14.6 %multiply_reduce_fusion = (f32[32,64]{1,0:T(8,128)}, f32[8,32]{1,0:T(8,128)S(1)}, f32[8,121,32,64]{1,3,2,0:T(8,128)S(1)}) fusion(f32[32,64]{1,0:T(8,128)S(1)} %slice.135, f32[8,121,32,64]{1,3,2,0:T(8,128)} %copy-done.1, f32[8,32]{1,0:T(8,128)S(1)} %broadcast_multiply_fusion.4, f32[8,32,64]{2,1,0:T(8,128)S(1)} %div.147, f32[8,32,64]{2,1,0:T(8,128)S(1)} %mul.761, ...), kind=kLoop, calls=%fused_computation.19 | loop fusion | flops 55506688 | bytes 23948288 | tf_op jit(solution)/shard_map/transpose(jvp())/reduce_sum | solution.py:51
  371.3 12.6 %copy.362 = bf16[8,121,32,16]{3,2,1,0:T(8,128)(2,1)} copy(bf16[8,121,32,16]{1,2,3,0:T(8,128)(2,1)S(1)} %add_convert_fusion.2) | data formatting | bytes 1982464 | tf_op jit(solution)/shard_map/convert_element_type | solution.py:143
  383.9 13.9 %reshape.570 = bf16[8,11,11,512]{3,2,1,0:T(8,128)(2,1)} reshape(bf16[8,121,32,16]{3,2,1,0:T(8,128)(2,1)} %copy.362) | data formatting | bytes 1982464 | tf_op jit(solution)/shard_map/convert_element_type | solution.py:143
  397.8 14.7 %fusion.17 = f32[8,11,11,4608]{3,2,1,0:T(8,128)} fusion(bf16[8,11,11,512]{3,2,1,0:T(8,128)(2,1)} %reshape.570, bf16[1,4608,512]{2,1,0:T(8,128)(2,1)} %all-gather.11.cloned.1.call-done), kind=kOutput, calls=%fused_computation.36 | convolution fusion | flops 4567597056 | bytes 23552000 | tf_op jit(solution)/shard_map/bpm,km->bpk/dot_general | solution.py:147
  412.5 18.2 %fusion.101 = (f32[8,11,11,512]{3,2,1,0:T(8,128)}, f32[8,11,11,512]{3,2,1,0:T(8,128)}, f32[8,11,11,512]{3,2,1,0:T(8,128)}, f32[8,11,11,512]{3,2,1,0:T(8,128)}, f...) fusion(f32[8,11,11,4608]{3,2,1,0:T(8,128)} %fusion.17), kind=kLoop, calls=%fused_computation.251 | loop fusion | bytes 35684352 | tf_op jit(solution)/shard_map/transpose(jvp())/split | solution.py:63
  494.0 14.7 %constant_dynamic-slice_fusion.1 = (f32[128,18360]{0,1:T(8,128)}, f32[128,18360]{0,1:T(8,128)}) fusion(f32[128,36720]{0,1:T(8,128)} %param.38, s32[]{:T(128)S(6)} %select_n.138, f32[128,36720]{0,1:T(8,128)} %param.33), kind=kLoop, calls=%fused_computation.193 | loop fusion | bytes 37601284 | tf_op jit(solution)/shard_map/dynamic_slice | solution.py:104
  517.4 22.6 %reshape.529 = f32[128,36720]{1,0:T(8,128)} reshape(f32[5120,918]{1,0:T(8,128)} %fusion.107) | data formatting | bytes 37601280 | tf_op jit(solution)/shard_map/reshape | solution.py:287
  555.7 11.8 %convolution_bitcast_fusion = f32[1,4608,512]{2,1,0:T(8,128)} fusion(bf16[8,121,4608]{2,1,0:T(8,128)(2,1)} %copy_dynamic-update-slice_fusion, bf16[8,121,512]{1,2,0:T(8,128)(2,1)S(1)} %bitcast.189), kind=kOutput, calls=%fused_computation.23 | convolution fusion | flops 4567597056 | bytes 19349504 | tf_op jit(solution)/shard_map/bpk,bpm->km/dot_general | solution.py:145
  606.9 29.2 %psum.14 = f32[40]{0:T(128)S(1)} all-reduce(f32[40]{0:T(128)S(1)} %convolution_bitcast_fusion.3), channel_id=1, replica_groups=mesh['role'=2,'dp'=16] {'dp'}, use_global_device_ids=true, to_apply=%region_22.23 | all-reduce | flops 40 | bytes 320 | tf_op jit(solution)/shard_map/psum | solution.py:254
  641.3 18.4 %collective-permute-done.1 = bf16[]{:T(256)} collective-permute-done((bf16[]{:T(256)}, bf16[]{:T(256)}, u32[]{:S(2)}, u32[]{:S(2)}) %collective-permute-start.1) | collective-permute-done | bytes 34 | tf_op jit(solution)/shard_map/ppermute | solution.py:31
  668.8 21.0 %fusion.94 = (bf16[128,18360]{1,0:T(8,128)(2,1)}, f32[128,18360]{1,0:T(8,128)}, f32[128,18360]{1,0:T(8,128)}) fusion(f32[128,18360]{1,0:T(8,128)} %copy.369, bf16[128,18360]{1,0:T(8,128)(2,1)} %copy.340, f32[128,36720]{1,0:T(8,128)} %reshape.529, pred[]{:T(512)S(6)} %eq.74, f32[128,18360]{1,0:T(8,128)} %copy.370), kind=kLoop, calls=%fused_computation.246 | loop fusion | flops 21150720 | bytes 56401920 | tf_op jit(solution)/shard_map/convert_element_type | solution.py:91
  692.1 11.2 %add_multiply_fusion = f32[128,18360]{1,0:T(8,128)} fusion(f32[128,18360]{1,0:T(8,128)} %copy.371, f32[128,18360]{1,0:T(8,128)} %get-tuple-element.166), kind=kLoop, calls=%fused_computation.10 | loop fusion | flops 4700160 | bytes 28200960 | tf_op jit(solution)/shard_map/add | solution.py:90
  750.5 59.0 %reduce-scatter.12.cloned.1.call-done = f32[1,288,512]{2,1,0:T(8,128)} async-done(((f32[1,4608,512]{2,1,0:T(8,128)}), f32[1,288,512]{2,1,0:T(8,128)}) %reduce-scatter.12.cloned.1.call-update) | async-done | bytes 589840 | tf_op jit(solution)/shard_map/reduce_scatter | solution.py:286
  (357 shorter events, 336.5 us)
Async XLA Ops:
  7.2 561.4 %copy-start = (f32[1,128,512]{2,1,0:T(8,128)S(1)}, f32[1,128,512]{2,1,0:T(8,128)}, u32[]{:S(2)}) copy-start(f32[1,128,512]{2,1,0:T(8,128)} %param.34) | copy-start | bytes 786436
  7.2 123.6 %all-gather.9.cloned.1.call-start = ((), (), s32[]{:S(2)}) async-start(), calls=%async_computation.10 | async-start | bytes 2228224 | tf_op jit(solution)/shard_map/all_gather | solution.py:201
  8.9 131.8 %all-gather.13.cloned.1.call-start = ((), (), s32[]{:S(2)}) async-start(), calls=%async_computation.12 | async-start | bytes 2228224 | tf_op jit(solution)/shard_map/all_gather | solution.py:203
  10.7 147.9 %all-gather.11.cloned.1.call-start = ((), (), s32[]{:S(2)}) async-start(), calls=%async_computation.11 | async-start | bytes 5013504 | tf_op jit(solution)/shard_map/all_gather | solution.py:202
  12.6 274.4 %reduce-scatter.8.cloned.1.call-start = ((), (), s32[]{:S(2)}) async-start(), calls=%async_computation.6 | async-start | bytes 557056 | tf_op jit(solution)/shard_map/reduce_scatter | solution.py:231
  130.6 313.3 %copy-start.34 = (f32[1,512]{1,0:T(1,128)}, f32[1,512]{1,0:T(1,128)S(1)}, u32[]{:S(2)}) copy-start(f32[1,512]{1,0:T(1,128)S(1)} %get-tuple-element.208) | copy-start | bytes 6148
  139.2 304.7 %copy-start.27 = (f32[8,512]{1,0:T(8,128)}, f32[8,512]{1,0:T(8,128)S(1)}, u32[]{:S(2)}) copy-start(f32[8,512]{1,0:T(8,128)S(1)} %mul.687) | copy-start | bytes 49156
  289.9 3.8 collective-permute-start
  320.0 13.1 %all-to-all-start = ((bf16[16,8,128]{2,1,0:T(8,128)(2,1)}), bf16[16,8,128]{2,1,0:T(8,128)(2,1)S(1)}, u32[]{:S(2)}, u32[]{:S(2)}) async-start(bf16[16,8,128]{2,1,0:T(8,128)(2,1)} %bitcast.131), calls=%async_computation.1 | async-start | bytes 65536 | tf_op jit(solution)/shard_map/all_to_all | solution.py:273
  325.6 310.5 %reduce-scatter.16.cloned.1.call-start = ((), (), s32[]{:S(2)}) async-start(), calls=%async_computation.13 | async-start | bytes 3342336
  475.1 214.8 %reduce-scatter.10.cloned.1.call-start = ((), (), s32[]{:S(2)}) async-start(), calls=%async_computation.7 | async-start | bytes 4456448 | tf_op jit(solution)/shard_map/reduce_scatter | solution.py:286
  486.0 254.2 %reduce-scatter.14.cloned.1.call-start = ((), (), s32[]{:S(2)}) async-start(), calls=%async_computation.9 | async-start | bytes 4456448 | tf_op jit(solution)/shard_map/reduce_scatter | solution.py:286
  493.9 315.5 %reduce-scatter.12.cloned.1.call-start = ((), (), s32[]{:S(2)}) async-start(), calls=%async_computation.8 | async-start | bytes 10027008 | tf_op jit(solution)/shard_map/reduce_scatter | solution.py:286
  554.0 108.3 %collective-permute-start.6 = (bf16[128,18360]{0,1:T(8,128)(2,1)}, bf16[128,18360]{0,1:T(8,128)(2,1)}, u32[]{:S(2)}, u32[]{:S(2)}) collective-permute-start(bf16[128,18360]{0,1:T(8,128)(2,1)} %copy.339), channel_id=1, source_target_pairs={{0,16},{1,17},{2,18},{3,19},{4,20},{5,21},{6,22},{7,23},{8,24},{9,... | collective-permute-start | bytes 14100488 | tf_op jit(solution)/shard_map/ppermute | solution.py:31
  637.2 23.9 %collective-permute-start.5 = (bf16[1,384]{1,0:T(2,128)(2,1)S(1)}, bf16[1,384]{1,0:T(2,128)(2,1)S(1)}, u32[]{:S(2)}, u32[]{:S(2)}) collective-permute-start(bf16[1,384]{1,0:T(2,128)(2,1)S(1)} %convert_element_type.224), channel_id=1, source_target_pairs={{0,16},{1,17},{2,18},{3,19},{4,20},{5,21},{6,22},{7,23},{8,24},{9,... | collective-permute-start | bytes 2312 | tf_op jit(solution)/shard_map/ppermute | solution.py:31
  639.8 20.0 %collective-permute-start.1 = (bf16[]{:T(256)}, bf16[]{:T(256)}, u32[]{:S(2)}, u32[]{:S(2)}) collective-permute-start(bf16[]{:T(256)} %convert_element_type.203), channel_id=1, source_target_pairs={{0,16},{1,17},{2,18},{3,19},{4,20},{5,21},{6,22},{7,23},{8,24},{9,... | collective-permute-start | bytes 14 | tf_op jit(solution)/shard_map/ppermute | solution.py:31
  690.8 52.4 %collective-permute-start.2 = (bf16[1,128,256]{1,2,0:T(8,128)(2,1)S(1)}, bf16[1,128,256]{1,2,0:T(8,128)(2,1)}, u32[]{:S(2)}, u32[]{:S(2)}) collective-permute-start(bf16[1,128,256]{1,2,0:T(8,128)(2,1)S(1)} %slice.200), channel_id=1, source_target_pairs={{0,16},{1,17},{2,18},{3,19},{4,20},{5,21},{6,22},{7,23},{8,24},{9,... | collective-permute-start | bytes 196616 | tf_op jit(solution)/shard_map/ppermute | solution.py:31
  740.2 71.6 %copy-start.24 = (f32[1,32,2048]{2,1,0:T(8,128)S(1)}, f32[1,32,2048]{2,1,0:T(8,128)}, u32[]{:S(2)}) copy-start(f32[1,32,2048]{2,1,0:T(8,128)} %param.41) | copy-start | bytes 786436
  740.2 77.7 %copy-start.16 = (f32[1,288,512]{2,1,0:T(8,128)S(1)}, f32[1,288,512]{2,1,0:T(8,128)}, u32[]{:S(2)}) copy-start(f32[1,288,512]{2,1,0:T(8,128)} %param.30) | copy-start | bytes 1769476
  740.2 77.7 %copy-start.29 = (f32[1,288,512]{2,1,0:T(8,128)S(1)}, f32[1,288,512]{2,1,0:T(8,128)}, u32[]{:S(2)}) copy-start(f32[1,288,512]{2,1,0:T(8,128)} %param.35) | copy-start | bytes 1769476
  740.2 79.5 %copy-start.15 = (f32[1,288,512]{2,1,0:T(8,128)S(1)}, f32[1,288,512]{2,1,0:T(8,128)}, u32[]{:S(2)}) copy-start(f32[1,288,512]{2,1,0:T(8,128)} %param.40) | copy-start | bytes 1769476
  741.9 6.9 collective-permute-start.4
  750.5 70.0 %copy-start.26 = (f32[1,32,1024]{2,1,0:T(8,128)}, f32[1,32,1024]{2,1,0:T(8,128)S(1)}, u32[]{:S(2)}) copy-start(f32[1,32,1024]{2,1,0:T(8,128)S(1)} %get-tuple-element.172) | copy-start | bytes 393220
  810.5 7.4 collective-permute-start.3
  (58 other events, 996.1 us)
Sparse Core Ops, SparseCore 0:
  10.8 41.6 all-gather.8
  55.2 40.1 all-gather.12
  98.3 52.0 all-gather.10
  232.3 54.6 reduce-scatter.7
  475.2 67.4 reduce-scatter.15
  546.9 71.3 reduce-scatter.9
  622.2 71.3 reduce-scatter.13
  698.3 111.1 reduce-scatter.11
where the time goes:
time: 842 us; the launch traced here: 829 us
  local copies, waits for them, and re-layouts  304 us (36%)
  blocking collectives  145 us (17%)
  other arithmetic  140 us (17%)
  waiting for transfers between devices  112 us (13%)
  matrix products  92 us (11%)
  between operations  19.5 us (2%)
  starting transfers between devices  16.6 us (2%)
    unnamed x163, local copies, waits for them, and re-layouts  93.7 us
    reduce_scatter x3, waiting for transfers between devices, on_device(): reduced = lax.psum_scatter(stacked, 'dp', scatter_dimension=1, tiled=True)  59 us
    psum x2, blocking collectives, on_device(): total_counts, total_sums = lax.psum((counts, sums), 'dp')  56.3 us
    reduce_sum x4, other arithmetic, group_norm(): return normed * gain + shift  30.8 us
    unnamed x1, blocking collectives  29.1 us
    reduce_scatter x1, waiting for transfers between devices, on_device(): lax.psum_scatter(jnp.dot(spread_rows, head_low, preferred_element_type=jn...  27.2 us
    convert_element_type x3, local copies, waits for them, and re-layouts, block_backward(): d_two = d_two.astype(jnp.bfloat16)  27 us
    convert_element_type x5, other arithmetic, renew(): new_weight.astype(jnp.bfloat16)  26 us
  transfers between devices with their start and end apart: 16, of which 6 were waited for; matrix products, arithmetic and copies ran while one was open for 39% of the time, Pallas kernels for 0%

commit v1 on v0

--- a/solution.py
+++ b/solution.py
@@ -1,6 +1,11 @@
+import functools
+
 import jax
 import jax.numpy as jnp
+import numpy as np
 from jax import lax
+from jax.experimental import pallas as pl
+from jax.experimental.pallas import tpu as pltpu
 from jax.sharding import PartitionSpec as P
 
 D = 2048
@@ -355,9 +360,1036 @@
     )
 
 
+D = 2048
+MID = 512
+GROUPS = 32
+SIDE = 11
+PIX = 121
+TB = 8
+PITCH = 12
+RB = PITCH * TB
+VR = SIDE * TB
+ROWS = SIDE * RB
+PAD = 16 * TB
+EROWS = 164 * TB
+BLK = 352
+CH = 512
+epsilon = 1e-05
+GK = 0.7978845608028654
+GC = 0.044715
+OFFS = [(i - 1) * PITCH + (j - 1) for i in range(3) for j in range(3)]
+
+
+def group_sum(v, gs):
+    width = v.shape[1]
+    n = width // 128
+    a = lax.broadcasted_iota(jnp.int32, (128, 128), 0) // gs
+    b = lax.broadcasted_iota(jnp.int32, (128, 128), 1) // gs
+    m = (a == b).astype(jnp.float32)
+    st = jnp.concatenate([v[:, k * 128:(k + 1) * 128] for k in range(n)], axis=0)
+    r = jnp.dot(st, m, precision=lax.Precision.HIGHEST, preferred_element_type=jnp.float32)
+    return jnp.concatenate([r[k * 8:(k + 1) * 8] for k in range(n)], axis=1)
+
+
+def fold(v):
+    rows, w = v.shape
+    return jnp.sum(v.reshape(rows // TB, TB, w), axis=0)
+
+
+def moments(h_ref, lo, gs):
+    def one(r, acc):
+        return acc + fold(h_ref[pl.ds(pl.multiple_of(r * RB, RB), VR), lo:lo + CH])
+    s = lax.fori_loop(0, SIDE, one, jnp.zeros((TB, CH), jnp.float32))
+    mean = group_sum(s, gs) / float(PIX * gs)
+
+    def two(r, acc):
+        h = h_ref[pl.ds(pl.multiple_of(r * RB, RB), VR), lo:lo + CH].reshape(SIDE, TB, CH) - mean[None]
+        return acc + jnp.sum(h * h, axis=0)
+    q = lax.fori_loop(0, SIDE, two, jnp.zeros((TB, CH), jnp.float32))
+    var = group_sum(q, gs) / float(PIX * gs)
+    return mean, lax.rsqrt(var + epsilon)
+
+
+def gelu(u):
+    return 0.5 * u * (1.0 + jnp.tanh(GK * (u + GC * (u * u * u))))
+
+
+def dgelu(u):
+    uu = u * u
+    t = jnp.tanh(GK * u * (1.0 + GC * uu))
+    return 0.5 * (1.0 + t) + 0.5 * u * (1.0 - t * t) * (GK + (3.0 * GK * GC) * uu)
+
+
+def shifted(e_ref, o_ref, s, row, n):
+    ref, base = (e_ref, 16 + s) if s % 2 == 0 else (o_ref, 17 + s)
+    return ref[pl.ds(pl.multiple_of(row + base * TB, 16), n), :]
+
+
+def put_shifted(e_ref, o_ref, r, v):
+    z = jnp.zeros((TB, v.shape[1]), jnp.float32)
+    at = pl.ds(pl.multiple_of(PAD + r * RB, 16), RB)
+    e_ref[at, :] = jnp.concatenate([v, z], axis=0).astype(jnp.bfloat16)
+    o_ref[at, :] = jnp.concatenate([z, v], axis=0).astype(jnp.bfloat16)
+
+
+def clear_margins(e_ref, o_ref):
+    z = jnp.zeros((PAD, MID), jnp.bfloat16)
+    for ref in (e_ref, o_ref):
+        ref[0:PAD, :] = z
+        ref[PAD + ROWS:EROWS, :] = z
+
+
+def row_at(r):
+    return pl.ds(pl.multiple_of(r * RB, RB), VR)
+
+
+def rows_full(r):
+    return pl.ds(pl.multiple_of(r * RB, RB), RB)
+
+
+def fwd_kernel(fr_ref, win_ref, wmid_ref, wout_ref, g_ref, x_ref, h1_ref, h2_ref, h3_ref, a1_ref, a2_ref, st_ref,
+               feat_ref, e_ref, o_ref):
+    def place_row(r, c):
+        v = fr_ref[pl.ds(r * SIDE, SIDE)].astype(jnp.float32).reshape(VR, D)
+        z = jnp.zeros((TB, D), jnp.float32)
+        x_ref[rows_full(r), :] = jnp.concatenate([v, z], axis=0).astype(jnp.bfloat16)
+        return c
+    lax.fori_loop(0, SIDE, place_row, 0)
+    clear_margins(e_ref, o_ref)
+
+    def mm1(i, c):
+        rs = pl.ds(pl.multiple_of(i * BLK, BLK), BLK)
+        h1_ref[rs, :] = jnp.dot(x_ref[rs, :], win_ref[...], preferred_element_type=jnp.float32)
+        return c
+    lax.fori_loop(0, ROWS // BLK, mm1, 0)
+    mean, rstd = moments(h1_ref, 0, MID // GROUPS)
+    st_ref[0:8, 0:MID] = mean
+    st_ref[8:16, 0:MID] = rstd
+    sc = rstd * g_ref[:, 0:MID]
+    sh = g_ref[:, MID:2 * MID] - mean * sc
+
+    def act1(r, c):
+        h = h1_ref[row_at(r), :].reshape(SIDE, TB, MID)
+        a = gelu(h * sc[None] + sh[None]).reshape(VR, MID)
+        put_shifted(e_ref, o_ref, r, a)
+        return c
+    lax.fori_loop(0, SIDE, act1, 0)
+    a1_ref[...] = e_ref[PAD:PAD + ROWS, :]
+
+    def mm2(i, c):
+        row = i * BLK
+        acc = None
+        for n, s in enumerate(OFFS):
+            p = jnp.dot(shifted(e_ref, o_ref, s, row, BLK), wmid_ref[n * MID:(n + 1) * MID, :],
+                        preferred_element_type=jnp.float32)
+            acc = p if acc is None else acc + p
+        h2_ref[pl.ds(pl.multiple_of(row, BLK), BLK), :] = acc
+        return c
+    lax.fori_loop(0, ROWS // BLK, mm2, 0)
+    mean, rstd = moments(h2_ref, 0, MID // GROUPS)
+    st_ref[0:8, MID:2 * MID] = mean
+    st_ref[8:16, MID:2 * MID] = rstd
+    sc2 = rstd * g_ref[:, 2 * MID:3 * MID]
+    sh2 = g_ref[:, 3 * MID:4 * MID] - mean * sc2
+
+    def act2(r, c):
+        h = h2_ref[rows_full(r), :].reshape(PITCH, TB, MID)
+        a2_ref[rows_full(r), :] = gelu(h * sc2[None] + sh2[None]).reshape(RB, MID).astype(jnp.bfloat16)
+        return c
+    lax.fori_loop(0, SIDE, act2, 0)
+
+    def mm3(i, c):
+        rs = pl.ds(pl.multiple_of(i * BLK, BLK), BLK)
+        h3_ref[rs, :] = jnp.dot(a2_ref[rs, :], wout_ref[...], preferred_element_type=jnp.float32)
+        return c
+    lax.fori_loop(0, ROWS // BLK, mm3, 0)
+    for k in range(D // CH):
+        lo = k * CH
+        mean, rstd = moments(h3_ref, lo, D // GROUPS)
+        st_ref[0:8, 2 * MID + lo:2 * MID + lo + CH] = mean
+        st_ref[8:16, 2 * MID + lo:2 * MID + lo + CH] = rstd
+        sc3 = rstd * g_ref[:, 4 * MID + lo:4 * MID + lo + CH]
+        sh3 = g_ref[:, 4 * MID + D + lo:4 * MID + D + lo + CH] - mean * sc3
+
+        def act3(r, acc):
+            h = h3_ref[row_at(r), lo:lo + CH].reshape(SIDE, TB, CH)
+            s = x_ref[rows_full(r), lo:lo + CH].astype(jnp.float32)[0:VR].reshape(SIDE, TB, CH)
+            return acc + jnp.sum(gelu(s + (h * sc3[None] + sh3[None])), axis=0)
+        acc = lax.fori_loop(0, SIDE, act3, jnp.zeros((TB, CH), jnp.float32))
+        feat_ref[:, lo:lo + CH] = (acc / float(PIX)).astype(jnp.bfloat16).astype(jnp.float32)
+
+
+def VS():
+    return pl.BlockSpec(memory_space=pltpu.VMEM)
+
+
+def forward(frames, w_in, w_mid, w_out, gains):
+    f32, b16 = jnp.float32, jnp.bfloat16
+    S = jax.ShapeDtypeStruct
+    return pl.pallas_call(
+        fwd_kernel,
+        out_shape=(S((ROWS, D), b16), S((ROWS, MID), f32), S((ROWS, MID), f32), S((ROWS, D), f32), S((ROWS, MID), b16),
+                   S((ROWS, MID), b16), S((16, 2 * MID + D), f32), S((TB, D), f32)),
+        in_specs=[VS()] * 5,
+        out_specs=(VS(),) * 8,
+        scratch_shapes=[pltpu.VMEM((EROWS, MID), b16), pltpu.VMEM((EROWS, MID), b16)],
+        compiler_params=pltpu.CompilerParams(vmem_limit_bytes=60 * 1024 * 1024),
+        name="block_forward",
+    )(frames, w_in, w_mid, w_out, gains)
+
+
+def norm_back(h_ref, dy_ref, lo, mean, rstd, gain, gs, s1, s2, emit):
+    n = 1.0 / float(PIX * gs)
+    m1 = group_sum(gain * s1, gs) * n
+    m2 = group_sum(gain * s2, gs) * n
+    ca = rstd * gain
+    cc = -rstd * rstd * m2
+    cb = -rstd * m1 - mean * cc
+
+    def one(r, c):
+        h = h_ref[row_at(r), lo:lo + CH].reshape(SIDE, TB, CH)
+        dy = dy_ref[row_at(r), lo:lo + CH].reshape(SIDE, TB, CH)
+        emit(r, (ca[None] * dy + cc[None] * h + cb[None]).reshape(VR, CH))
+        return c
+    lax.fori_loop(0, SIDE, one, 0)
+
+
+def bwd_kernel(dfeat_ref, x_ref, h1_ref, h2_ref, h3_ref, a1_ref, a2_ref, st_ref, wmid_ref, wout_ref, g_ref, gin_ref,
+               gmid_ref, gout_ref, gg_ref, du_ref, dh3_ref, d2_ref, e_ref, o_ref, dh1_ref):
+    T0 = (((0,), (0,)), ((), ()))
+    T1 = (((1,), (1,)), ((), ()))
+    clear_margins(e_ref, o_ref)
+    z8 = jnp.zeros((TB, CH), jnp.float32)
+
+    def put_gain(at, s):
+        gg_ref[:, at:at + CH] = jnp.sum(s, axis=0, keepdims=True)
+
+    for k in range(D // CH):
+        lo = k * CH
+        mean = st_ref[0:8, 2 * MID + lo:2 * MID + lo + CH]
+        rstd = st_ref[8:16, 2 * MID + lo:2 * MID + lo + CH]
+        gain = g_ref[:, 4 * MID + lo:4 * MID + lo + CH]
+        shift = g_ref[:, 4 * MID + D + lo:4 * MID + D + lo + CH]
+        dout = dfeat_ref[:, lo:lo + CH] / float(PIX)
+        mr = mean * rstd
+
+        def one(r, acc):
+            s1, s2 = acc
+            h = h3_ref[row_at(r), lo:lo + CH].reshape(SIDE, TB, CH)
+            s = x_ref[rows_full(r), lo:lo + CH].astype(jnp.float32)[0:VR].reshape(SIDE, TB, CH)
+            xh = h * rstd[None] - mr[None]
+            du = dout[None] * dgelu(s + (xh * gain + shift))
+            du_ref[row_at(r), :] = du.reshape(VR, CH)
+            return s1 + jnp.sum(du, axis=0), s2 + jnp.sum(du * xh, axis=0)
+        s1, s2 = lax.fori_loop(0, SIDE, one, (z8, z8))
+        put_gain(4 * MID + lo, s2)
+        put_gain(4 * MID + D + lo, s1)
+        gs = D // GROUPS
+        n = 1.0 / float(PIX * gs)
+        m1 = group_sum(gain * s1, gs) * n
+        m2 = group_sum(gain * s2, gs) * n
+        ca = rstd * gain
+        cc = -rstd * rstd * m2
+        cb = -rstd * m1 - mean * cc
+
+        def two(r, c):
+            h = h3_ref[row_at(r), lo:lo + CH].reshape(SIDE, TB, CH)
+            dy = du_ref[row_at(r), :].reshape(SIDE, TB, CH)
+            v = (ca[None] * dy + cc[None] * h + cb[None]).reshape(VR, CH)
+            dh3_ref[rows_full(r), lo:lo + CH] = jnp.concatenate([v, z8], axis=0).astype(jnp.bfloat16)
+            return c
+        lax.fori_loop(0, SIDE, two, 0)
+        gout_ref[:, lo:lo + CH] = lax.dot_general(a2_ref[...], dh3_ref[:, lo:lo + CH], T0,
+                                                  preferred_element_type=jnp.float32)
+
+    def da2(i, c):
+        rs = pl.ds(pl.multiple_of(i * BLK, BLK), BLK)
+        d2_ref[rs, :] = lax.dot_general(dh3_ref[rs, :], wout_ref[...], T1, preferred_element_type=jnp.float32)
+        return c
+    lax.fori_loop(0, ROWS // BLK, da2, 0)
+
+    def through(h_ref, at, goff, boff, emit):
+        mean = st_ref[0:8, at:at + MID]
+        rstd = st_ref[8:16, at:at + MID]
+        gain = g_ref[:, goff:goff + MID]
+        shift = g_ref[:, boff:boff + MID]
+        mr = mean * rstd
+
+        def one(r, acc):
+            s1, s2 = acc
+            h = h_ref[row_at(r), :].reshape(SIDE, TB, MID)
+            da = d2_ref[row_at(r), :].reshape(SIDE, TB, MID)
+            xh = h * rstd[None] - mr[None]
+            dy = da * dgelu(xh * gain + shift)
+            d2_ref[row_at(r), :] = dy.reshape(VR, MID)
+            return s1 + jnp.sum(dy, axis=0), s2 + jnp.sum(dy * xh, axis=0)
+        s1, s2 = lax.fori_loop(0, SIDE, one, (z8, z8))
+        put_gain(goff, s2)
+        put_gain(boff, s1)
+        norm_back(h_ref, d2_ref, 0, mean, rstd, gain, MID // GROUPS, s1, s2, emit)
+
+    through(h2_ref, MID, 2 * MID, 3 * MID, lambda r, v: put_shifted(e_ref, o_ref, r, v))
+    for n, s in enumerate(OFFS):
+        gmid_ref[n * MID:(n + 1) * MID, :] = lax.dot_general(
+            a1_ref[...], shifted(e_ref, o_ref, -s, 0, ROWS), T0, preferred_element_type=jnp.float32)
+
+    def da1(i, c):
+        row = i * BLK
+        acc = None
+        for n, s in enumerate(OFFS):
+            p = lax.dot_general(shifted(e_ref, o_ref, -s, row, BLK), wmid_ref[n * MID:(n + 1) * MID, :], T1,
+                                preferred_element_type=jnp.float32)
+            acc = p if acc is None else acc + p
+        d2_ref[pl.ds(pl.multiple_of(row, BLK), BLK), :] = acc
+        return c
+    lax.fori_loop(0, ROWS // BLK, da1, 0)
+
+    def put1(r, v):
+        dh1_ref[rows_full(r), :] = jnp.concatenate([v, z8], axis=0).astype(jnp.bfloat16)
+    through(h1_ref, 0, 0, MID, put1)
+
+    for k in range(D // CH):
+        gin_ref[k * CH:(k + 1) * CH, :] = lax.dot_general(x_ref[:, k * CH:(k + 1) * CH], dh1_ref[...], T0,
+                                                          preferred_element_type=jnp.float32)
+
+
+def backward(dfeat, saved, w_mid, w_out, gains):
+    f32, b16 = jnp.float32, jnp.bfloat16
+    S = jax.ShapeDtypeStruct
+    x, h1, h2, h3, a1, a2, st, feat = saved
+    V = pltpu.VMEM
+    return pl.pallas_call(
+        bwd_kernel,
+        out_shape=(S((D, MID), f32), S((9 * MID, MID), f32), S((MID, D), f32), S((1, 4 * MID + 2 * D), f32)),
+        in_specs=[VS()] * 11,
+        out_specs=(VS(),) * 4,
+        scratch_shapes=[V((ROWS, CH), f32), V((ROWS, D), b16), V((ROWS, MID), f32), V((EROWS, MID), b16),
+                        V((EROWS, MID), b16), V((ROWS, MID), b16)],
+        compiler_params=pltpu.CompilerParams(vmem_limit_bytes=62 * 1024 * 1024),
+        name="block_backward",
+    )(dfeat, x, h1, h2, h3, a1, a2, st, w_mid, w_out, gains)
+
+
+MESH = pl.DeviceIdType.MESH
+
+
+def any_spec():
+    return pl.BlockSpec(memory_space=pl.ANY)
+
+
+def greet(peers):
+    barrier = pltpu.get_barrier_semaphore()
+    for cond, dev in peers:
+        def go(dev=dev):
+            pl.semaphore_signal(barrier, inc=1, device_id=dev, device_id_type=MESH)
+        go() if cond is None else pl.when(cond)(go)
+    count = sum(1 for cond, _ in peers if cond is None)
+    for cond, _ in peers:
+        if cond is not None:
+            count = count + cond.astype(jnp.int32)
+    pl.semaphore_wait(barrier, count)
+
+
+def place():
+    me = lax.axis_index("dp")
+    core = lax.rem(me, 2)
+    x = lax.rem(me // 2, 2)
+    z = me // 4
+    return me, z, x, core
+
+
+def gather_kernel(nz, na, *refs):
+    ins, outs = refs[:na], refs[na:2 * na]
+    own_sem, send, recv = refs[2 * na:]
+    me, z, x, c = place()
+    up, down = {"dp": me + 4}, {"dp": me - 4}
+    xp = {"dp": me + 2 - 4 * x}
+    cp = {"dp": me + 1 - 2 * c}
+    has_up, has_down = z < nz - 1, z > 0
+    greet([(has_up, up), (has_down, down), (None, xp), (None, cp)])
+
+    def slot_of(zz, xx, cc):
+        return zz * 4 + xx * 2 + cc
+
+    started = []
+
+    def send_to(cond, a, src, slot, dev, k):
+        d = pltpu.make_async_remote_copy(src_ref=src, dst_ref=outs[a].at[slot], send_sem=send.at[a, k],
+                                         recv_sem=recv.at[a, slot], device_id=dev, device_id_type=MESH)
+        if cond is None:
+            d.start()
+        else:
+            pl.when(cond)(d.start)
+        started.append((cond, d))
+
+    def wait_for(cond, a, slot):
+        d = pltpu.make_async_remote_copy(src_ref=outs[a].at[slot], dst_ref=outs[a].at[slot], send_sem=send.at[a, 0],
+                                         recv_sem=recv.at[a, slot], device_id=cp, device_id_type=MESH)
+        if cond is None:
+            d.wait_recv()
+        else:
+            pl.when(cond)(d.wait_recv)
+
+    locals_ = []
+    for a in range(na):
+        send_to(has_up, a, ins[a], me, up, 0)
+        send_to(has_down, a, ins[a], me, down, 1)
+        send_to(None, a, ins[a], me, xp, 2)
+        send_to(None, a, ins[a], me, cp, 3)
+        l = pltpu.make_async_copy(ins[a], outs[a].at[me], own_sem.at[a])
+        l.start()
+        locals_.append(l)
+    for d in range(1, nz):
+        for a in range(na):
+            k = 4 + (d - 1) * 6
+            zb, za = z - d, z + d
+            ok_b, ok_a = zb >= 0, za < nz
+            sb, sa = me - 4 * d, me + 4 * d
+            wait_for(ok_b, a, sb)
+            send_to(jnp.logical_and(ok_b, has_up), a, outs[a].at[sb], sb, up, k)
+            send_to(ok_b, a, outs[a].at[sb], sb, xp, k + 1)
+            send_to(ok_b, a, outs[a].at[sb], sb, cp, k + 2)
+            wait_for(ok_a, a, sa)
+            send_to(jnp.logical_and(ok_a, has_down), a, outs[a].at[sa], sa, down, k + 3)
+            send_to(ok_a, a, outs[a].at[sa], sa, xp, k + 4)
+            send_to(ok_a, a, outs[a].at[sa], sa, cp, k + 5)
+    k = 4 + (nz - 1) * 6
+    for d in range(nz):
+        for a in range(na):
+            for sgn in ((1,) if d == 0 else (-1, 1)):
+                zz = z + sgn * d
+                ok = None if d == 0 else jnp.logical_and(zz >= 0, zz < nz)
+                s = slot_of(zz, 1 - x, c)
+                wait_for(ok, a, s)
+                send_to(ok, a, outs[a].at[s], s, cp, k + 2 * d + (1 if sgn > 0 else 0))
+    for d in range(nz):
+        for a in range(na):
+            for xx in (x, 1 - x):
+                for sgn in ((1,) if d == 0 else (-1, 1)):
+                    zz = z + sgn * d
+                    ok = None if d == 0 else jnp.logical_and(zz >= 0, zz < nz)
+                    wait_for(ok, a, slot_of(zz, xx, 1 - c))
+    for l in locals_:
+        l.wait()
+    for cond, d in started:
+        if cond is None:
+            d.wait_send()
+        else:
+            pl.when(cond)(d.wait_send)
+
+
+def gather(arrays, n, cid):
+    na = len(arrays)
+    nz = n // 4
+    return pl.pallas_call(
+        functools.partial(gather_kernel, nz, na),
+        out_shape=tuple(jax.ShapeDtypeStruct((n,) + a.shape, a.dtype) for a in arrays),
+        in_specs=[any_spec()] * na,
+        out_specs=(any_spec(),) * na,
+        scratch_shapes=[pltpu.SemaphoreType.DMA((na,)), pltpu.SemaphoreType.DMA((na, 4 + 6 * (nz - 1) + 2 * nz)),
+                        pltpu.SemaphoreType.DMA((na, n))],
+        compiler_params=pltpu.CompilerParams(collective_id=cid, has_side_effects=True),
+        name="weights_gather",
+    )(*arrays)
+
+
+def scatter_kernel(nz, na, *refs):
+    g, outs = refs[:na], refs[na:2 * na]
+    r1, r2, ru, rd, fs, fr = (refs[(2 + j) * na:(3 + j) * na] for j in range(6))
+    s1, q1, s2, q2, su, qu, sd, qd, sf, qf = refs[8 * na:]
+    me, z, x, c = place()
+    role = lax.axis_index("role")
+    up, down = {"dp": me + 4}, {"dp": me - 4}
+    xp = {"dp": me + 2 - 4 * x}
+    cp = {"dp": me + 1 - 2 * c}
+    has_up, has_down = z < nz - 1, z > 0
+    greet([(has_up, up), (has_down, down), (None, xp), (None, cp), (None, {"role": 1 - role})])
+
+    def rc(src, dst, ss, rs, dev):
+        return pltpu.make_async_remote_copy(src_ref=src, dst_ref=dst, send_sem=ss, recv_sem=rs, device_id=dev,
+                                            device_id_type=MESH)
+
+    def slot(zz, xx, cc):
+        return zz * 4 + xx * 2 + cc
+
+    order = list(range(nz))
+
+    def c1(a, zz, k):
+        xx = 1 - x if k == 0 else x
+        return rc(g[a].at[slot(zz, xx, 1 - c)], r1[a].at[k * nz + zz], s1.at[a, k * nz + zz], q1.at[a, k * nz + zz], cp)
+
+    def c2(a, zz):
+        return rc(g[a].at[slot(zz, 1 - x, c)], r2[a].at[zz], s2.at[a, zz], q2.at[a, zz], xp)
+
+    def cu(a, t):
+        return rc(g[a].at[slot(t, x, c)], ru[a].at[t], su.at[a, t], qu.at[a, t], up)
+
+    def cd(a, t):
+        return rc(g[a].at[slot(t, x, c)], rd[a].at[t], sd.at[a, t], qd.at[a, t], down)
+
+    def cf(a, to):
+        return rc(fs[a], fr[a], sf.at[a], qf.at[a], {"role": to})
+
+    @pl.when(role == 0)
+    def _():
+        for a in range(na):
+            for zz in order:
+                c1(a, zz, 0).start()
+            for zz in order:
+                c1(a, zz, 1).start()
+        for a in range(na):
+            for zz in order:
+                c1(a, zz, 0).wait_recv()
+                s = slot(zz, 1 - x, c)
+                g[a][s] = g[a][s] + r1[a][zz]
+                c2(a, zz).start()
+            for zz in order:
+                c1(a, zz, 1).wait_recv()
+                s = slot(zz, x, c)
+                g[a][s] = g[a][s] + r1[a][nz + zz]
+        for a in range(na):
+            for zz in order:
+                c2(a, zz).wait_recv()
+                s = slot(zz, x, c)
+                g[a][s] = g[a][s] + r2[a][zz]
+            for t in range(nz - 1, 0, -1):
+                @pl.when(z < t)
+                def _():
+                    @pl.when(z > 0)
+                    def _():
+                        cu(a, t).wait_recv()
+                        s = slot(t, x, c)
+                        g[a][s] = g[a][s] + ru[a][t]
+                    cu(a, t).start()
+                b = nz - 1 - t
+
+                @pl.when(z > b)
+                def _():
+                    @pl.when(z < nz - 1)
+                    def _():
+                        cd(a, b).wait_recv()
+                        s = slot(b, x, c)
+                        g[a][s] = g[a][s] + rd[a][b]
+                    cd(a, b).start()
+        for a in range(na):
+            @pl.when(z > 0)
+            def _():
+                cu(a, z).wait_recv()
+                g[a][me] = g[a][me] + ru[a][z]
+
+            @pl.when(z < nz - 1)
+            def _():
+                cd(a, z).wait_recv()
+                g[a][me] = g[a][me] + rd[a][z]
+            cols = outs[a].shape[1]
+            total = g[a][me]
+            outs[a][...] = total[:, :cols]
+            fs[a][...] = total[:, total.shape[1] - cols:].astype(fs[a].dtype)
+            cf(a, 1).start()
+        for a in range(na):
+            for zz in order:
+                c1(a, zz, 0).wait_send()
+                c1(a, zz, 1).wait_send()
+                c2(a, zz).wait_send()
+                pl.when(z < zz)(cu(a, zz).wait_send)
+                pl.when(z > zz)(cd(a, zz).wait_send)
+            cf(a, 1).wait_send()
+
+    @pl.when(role == 1)
+    def _():
+        for a in range(na):
+            cf(a, 0).wait_recv()
+            outs[a][...] = fr[a][...].astype(jnp.float32)
+
+
+def scatter(arrays, n, cid):
+    na = len(arrays)
+    nz = n // 4
+    V = pltpu.VMEM
+    sh = [a.shape[1:] for a in arrays]
+    half = [(s[0], s[1] // 2 if s[1] > 128 else s[1]) for s in sh]
+    low = [jnp.bfloat16 if s[1] > 128 else jnp.float32 for s in sh]
+    dt = jnp.float32
+    dma = pltpu.SemaphoreType.DMA
+    return pl.pallas_call(
+        functools.partial(scatter_kernel, nz, na),
+        out_shape=tuple(jax.ShapeDtypeStruct(s, dt) for s in half),
+        in_specs=[pl.BlockSpec(memory_space=pltpu.VMEM)] * na,
+        out_specs=(pl.BlockSpec(memory_space=pltpu.VMEM),) * na,
+        scratch_shapes=[V((2 * nz,) + s, dt) for s in sh] + [V((nz,) + s, dt) for s in sh] * 3 +
+        [V(s, t) for s, t in zip(half, low)] * 2 +
+        [dma((na, 2 * nz)), dma((na, 2 * nz))] + [dma((na, nz))] * 6 + [dma((na,))] * 2,
+        compiler_params=pltpu.CompilerParams(collective_id=cid, has_side_effects=True,
+                                             vmem_limit_bytes=62 * 1024 * 1024),
+        name="gradient_sums",
+    )(*arrays)
+
+
+D = 2048
+GAMES = 40
+ACTIONS = 18
+ATOMS = 51
+WIDE = ACTIONS * ATOMS
+LW = 1024
+WIN = 1024
+COLS = GAMES * WIDE
+HALF = COLS // 2
+PADC = 36864
+TB = 8
+support_low = -10.0
+support_high = 10.0
+discount = 0.99
+penalty = 0.05
+
+
+def window_of(g):
+    return (WIDE * g) // 16 * 16
+
+
+def ids_offset(ids):
+    return lax.bitwise_and(WIDE * ids, 15)
+
+
+def shift_rows(v, off, right):
+    width = v.shape[1]
+    for b in range(1, 4):
+        n = 1 << b
+        bit = lax.bitwise_and(off, n) != 0
+        bit = jnp.concatenate([bit.astype(jnp.float32)] * (width // 128), axis=1) > 0.5
+        v = jnp.where(bit, pltpu.roll(v, n if right else width - n, 1), v)
+    return v
+
+
+def head_kernel(n, feat_ref, gall_ref, scal_ref, head_ref, dfeat_ref, frow_ref, dlog_ref, loss_ref,
+                fsend, frecv, part, r1, r2, tgt_s, tgt_r, down_s, dsend, drecv,
+                s_f, q_f, s_1, q_1, s_2, q_2, s_t, q_t, s_l, q_l, s_c, q_c, s_d, q_d, s_r, q_r):
+    me, z, x, c = place()
+    role = lax.axis_index("role")
+    half = n // 2
+    peers = [lax.rem(me + k, n) for k in range(1, n)]
+    cp = me + 1 - 2 * c
+    greet([(None, {"dp": p}) for p in peers] + [(None, {"role": 1 - role})])
+
+    def rc(src, dst, ss, rs, dev):
+        return pltpu.make_async_remote_copy(src_ref=src, dst_ref=dst, send_sem=ss, recv_sem=rs, device_id=dev,
+                                            device_id_type=MESH)
+
+    for j in range(n):
+        fsend[j] = feat_ref[:, j * 128:(j + 1) * 128]
+    for k, p in enumerate(peers):
+        rc(fsend.at[p], frecv.at[me], s_f.at[k], q_f.at[me], {"dp": p}).start()
+    frecv[me] = fsend[me]
+    for k, p in enumerate(peers):
+        rc(fsend.at[p], frecv.at[p], s_f.at[k], q_f.at[p], {"dp": p}).wait_recv()
+    feats = frecv[...].reshape(n * TB, 128)
+    ids = gall_ref[...].reshape(n * TB, 128).astype(jnp.int32)
+
+    acc = None
+    for g in range(GAMES):
+        lhs = jnp.where(ids == g, feats, 0.0).astype(jnp.bfloat16)
+        a = window_of(g)
+        p = lax.dot_general(lhs, head_ref[a:a + WIN, :], (((1,), (1,)), ((), ())),
+                            preferred_element_type=jnp.float32)
+        acc = p if acc is None else acc + p
+    off = ids_offset(ids)
+    part[...] = shift_rows(acc, off, False).reshape(half, 2, TB, LW)
+
+    d1 = rc(part.at[:, 1 - c], r1, s_1, q_1, {"dp": cp})
+    d1.start()
+    d1.wait()
+    pair = me // 2
+    r1[...] = r1[...] + part[:, c]
+    pps = [lax.rem(pair + k, half) for k in range(1, half)]
+    for k, p in enumerate(pps):
+        rc(r1.at[p], r2.at[pair], s_2.at[k], q_2.at[pair], {"dp": 2 * p + c}).start()
+    r2[pair] = r1[pair]
+    for k, p in enumerate(pps):
+        rc(r1.at[p], r2.at[p], s_2.at[k], q_2.at[p], {"dp": 2 * p + c}).wait_recv()
+    logits = jnp.sum(r2[...], axis=0)
+
+    lane = lax.broadcasted_iota(jnp.int32, (TB, 128), 1)
+    live = lane < ATOMS
+    zi = support_low + (support_high - support_low) * lane.astype(jnp.float32) / (ATOMS - 1)
+    zi = jnp.where(live, zi, 0.0)
+    taken, nxt, expert, reward, done, gid = (scal_ref[k] for k in range(6))
+    pieces = []
+    for a in range(ACTIONS):
+        v = logits if a == 0 else pltpu.roll(logits, LW - ATOMS * a, 1)
+        pieces.append(v[:, :128])
+
+    @pl.when(role == 1)
+    def _():
+        sel = jnp.zeros((TB, 128), jnp.float32)
+        for a in range(ACTIONS):
+            sel = sel + jnp.where(nxt == float(a), pieces[a], 0.0)
+        sel = jnp.where(live, sel, -1e30)
+        e = jnp.exp(sel - jnp.max(sel, axis=1, keepdims=True))
+        e = jnp.where(live, e, 0.0)
+        prob = e / jnp.sum(e, axis=1, keepdims=True)
+        spacing = (support_high - support_low) / (ATOMS - 1)
+        m = jnp.zeros((TB, 128), jnp.float32)
+        for j in range(ATOMS):
+            zj = float(np.float32(support_low) + np.float32(support_high - support_low) * np.float32(j) /
+                       np.float32(ATOMS - 1))
+            tz = jnp.clip(reward + discount * (1.0 - done) * zj, support_low, support_high)
+            wt = jnp.maximum(0.0, 1.0 - jnp.abs(tz - zi) / spacing)
+            m = m + prob[:, j:j + 1] * wt
+        tgt_s[...] = jnp.where(live, m, 0.0)
+        d = rc(tgt_s, tgt_r, s_t, q_t, {"role": 0})
+        d.start()
+        d.wait_send()
+        rc(frow_ref, frow_ref, s_r.at[0], q_r.at[0], {"role": 0}).wait_recv()
+        rc(dlog_ref, dlog_ref, s_r.at[1], q_r.at[1], {"role": 0}).wait_recv()
+        dfeat_ref[...] = jnp.zeros_like(dfeat_ref)
+
+    @pl.when(role == 0)
+    def _():
+        frow_ref[...] = feats.astype(jnp.bfloat16)
+        gt = jnp.transpose(gall_ref[...].reshape(n * TB, 128))[0:TB]
+        count = jnp.sum((gt == gid).astype(jnp.float32), axis=1, keepdims=True)
+        weight = 1.0 / jnp.maximum(count, 1.0)
+        x3 = jnp.where(live[None], jnp.stack(pieces), -1e30)
+        act = lax.broadcasted_iota(jnp.int32, (ACTIONS, TB, 128), 0).astype(jnp.float32)
+        hot = (act == taken[None]).astype(jnp.float32)
+        mx = jnp.max(x3, axis=2, keepdims=True)
+        e = jnp.where(live[None], jnp.exp(x3 - mx), 0.0)
+        s = jnp.sum(e, axis=2, keepdims=True)
+        logp = jnp.where(live[None], x3 - mx - jnp.log(s), 0.0)
+        prob = e / s
+        q = jnp.sum(prob * zi[None], axis=2, keepdims=True)
+        qb = jnp.broadcast_to(q, (ACTIONS, TB, 128))
+        qm = jnp.max(qb, axis=0)
+        qe = jnp.exp(qb - qm[None])
+        qs = jnp.sum(qe, axis=0)
+        lse = qm + jnp.log(qs)
+        pol = qe / qs[None]
+        chosen = jnp.sum(logp * hot, axis=0)
+        qt = jnp.sum(qb * hot, axis=0)
+        rc(tgt_s, tgt_r, s_t, q_t, {"role": 1}).wait_recv()
+        m = tgt_r[...]
+        cross = -jnp.sum(m * chosen, axis=1, keepdims=True)
+        row_loss = cross + penalty * expert * (lse - qt)
+        msum = jnp.sum(m, axis=1, keepdims=True)
+        dl = hot * (prob * msum[None] - m[None]) + (penalty * expert)[None] * (pol - hot) * prob * (zi[None] - qb)
+        dl = jnp.where(live[None], dl * (weight * (1.0 / GAMES))[None], 0.0)
+        flat = jnp.zeros((TB, LW), jnp.float32)
+        pad = jnp.zeros((TB, LW - 128), jnp.float32)
+        for a in range(ACTIONS):
+            v = jnp.concatenate([dl[a], pad], axis=1)
+            flat = flat + (v if a == 0 else pltpu.roll(v, ATOMS * a, 1))
+        l0 = row_loss * weight
+        p0 = l0.astype(jnp.bfloat16).astype(jnp.float32)
+        p1 = (l0 - p0).astype(jnp.bfloat16).astype(jnp.float32)
+        p2 = l0 - p0 - p1
+        last = flat[:, LW - 128:]
+        last = jnp.where(lane == 125, p0, jnp.where(lane == 126, p1, jnp.where(lane == 127, p2, last)))
+        flat = jnp.concatenate([flat[:, :LW - 128], last], axis=1)
+        down_s[...] = jnp.concatenate([flat[:, :LW // 2], flat[:, LW // 2:]], axis=0).astype(jnp.bfloat16)
+        for k, p in enumerate(pps):
+            rc(down_s, dlog_ref.at[me], s_l.at[k], q_l.at[me], {"dp": 2 * p + c}).start()
+        rc(down_s, dlog_ref.at[me], s_c.at[0], q_c.at[me], {"dp": cp}).start()
+        dlog_ref[me] = down_s[...]
+        for k, p in enumerate(pps):
+            o = 2 * p + c
+            rc(down_s, dlog_ref.at[o], s_l.at[k], q_l.at[o], {"dp": cp}).wait_recv()
+            rc(dlog_ref.at[o], dlog_ref.at[o], s_c.at[k + 1], q_c.at[o], {"dp": cp}).start()
+        for p in [pair] + pps:
+            o = 2 * p + 1 - c
+            rc(dlog_ref.at[o], dlog_ref.at[o], s_c.at[0], q_c.at[o], {"dp": cp}).wait_recv()
+        to0 = rc(frow_ref, frow_ref, s_r.at[0], q_r.at[0], {"role": 1})
+        to1 = rc(dlog_ref, dlog_ref, s_r.at[1], q_r.at[1], {"role": 1})
+        to0.start()
+        to1.start()
+        rolled = shift_rows(widen(dlog_ref[...]), off, True)
+        acc = None
+        for g in range(GAMES):
+            lhs = jnp.where(jnp.concatenate([ids == g] * (WIN // 128), axis=1), rolled, 0.0).astype(jnp.bfloat16)
+            a = window_of(g)
+            p = jnp.dot(lhs, head_ref[a:a + WIN, :], preferred_element_type=jnp.float32)
+            acc = p if acc is None else acc + p
+        dsend[...] = acc.reshape(n, TB, 128)
+        for k, p in enumerate(peers):
+            rc(dsend.at[p], drecv.at[me], s_d.at[k], q_d.at[me], {"dp": p}).start()
+        drecv[me] = dsend[me]
+        for k, p in enumerate(peers):
+            rc(dsend.at[p], drecv.at[p], s_d.at[k], q_d.at[p], {"dp": p}).wait_recv()
+        for j in range(n):
+            dfeat_ref[:, j * 128:(j + 1) * 128] = drecv[j]
+        for k, p in enumerate(pps):
+            rc(down_s, dlog_ref.at[me], s_l.at[k], q_l.at[me], {"dp": 2 * p + c}).wait_send()
+        rc(down_s, dlog_ref.at[me], s_c.at[0], q_c.at[me], {"dp": cp}).wait_send()
+        for k, p in enumerate(pps):
+            o = 2 * p + c
+            rc(dlog_ref.at[o], dlog_ref.at[o], s_c.at[k + 1], q_c.at[o], {"dp": cp}).wait_send()
+        for k, p in enumerate(peers):
+            rc(dsend.at[p], drecv.at[me], s_d.at[k], q_d.at[me], {"dp": p}).wait_send()
+        to0.wait_send()
+        to1.wait_send()
+
+    for k, p in enumerate(peers):
+        rc(fsend.at[p], frecv.at[me], s_f.at[k], q_f.at[me], {"dp": p}).wait_send()
+    for k, p in enumerate(pps):
+        rc(r1.at[p], r2.at[pair], s_2.at[k], q_2.at[pair], {"dp": 2 * p + c}).wait_send()
+    tail = dlog_ref[:, :, 384:512].astype(jnp.float32)[:, TB:2 * TB].reshape(n * TB, 128)
+    lanes = lax.broadcasted_iota(jnp.int32, (n * TB, 128), 1)
+    total = jnp.sum(jnp.where(lanes >= 125, tail, 0.0))
+    loss_ref[...] = jnp.full((TB, 128), total, jnp.float32)
+
+
+def widen(dl):
+    n = dl.shape[0]
+    v = dl.astype(jnp.float32)
+    v = jnp.concatenate([v[:, 0:TB], v[:, TB:2 * TB]], axis=2).reshape(n * TB, LW)
+    lanes = lax.broadcasted_iota(jnp.int32, (n * TB, 128), 1)
+    last = jnp.where(lanes < WIDE - LW + 128, v[:, LW - 128:], 0.0)
+    return jnp.concatenate([v[:, :LW - 128], last], axis=1)
+
+
+def head_stage(feat, games_all, scal, head_low, n, cid):
+    f32, b16 = jnp.float32, jnp.bfloat16
+    S = jax.ShapeDtypeStruct
+    V, dma = pltpu.VMEM, pltpu.SemaphoreType.DMA
+    vs = pl.BlockSpec(memory_space=pltpu.VMEM)
+    h = n // 2
+    return pl.pallas_call(
+        functools.partial(head_kernel, n),
+        out_shape=(S((TB, D), f32), S((n * TB, 128), b16), S((n, 16, 512), b16), S((TB, 128), f32)),
+        in_specs=[vs] * 4,
+        out_specs=(vs,) * 4,
+        scratch_shapes=[V((n, TB, 128), f32), V((n, TB, 128), f32), V((h, 2, TB, LW), f32), V((h, TB, LW), f32),
+                        V((h, TB, LW), f32), V((TB, 128), f32), V((TB, 128), f32), V((16, 512), b16),
+                        V((n, TB, 128), f32), V((n, TB, 128), f32),
+                        dma((n,)), dma((n,)), dma, dma, dma((h,)), dma((h,)), dma, dma, dma((h,)), dma((n,)),
+                        dma((h,)), dma((n,)), dma((n,)), dma((n,)), dma((2,)), dma((2,))],
+        compiler_params=pltpu.CompilerParams(collective_id=cid, has_side_effects=True,
+                                             vmem_limit_bytes=56 * 1024 * 1024),
+        name="head_stage",
+    )(feat, games_all, scal, head_low)
+
+
+CR = 4096
+
+
+def cast_kernel(role_ref, h_ref, a_ref, o_ref):
+    rows = pl.program_id(0) * CR + lax.broadcasted_iota(jnp.int32, (256, 128), 0)
+
+    def fill(ref):
+        def one(r, c):
+            rs = pl.ds(pl.multiple_of(r * 256, 256), 256)
+            o_ref[rs, :] = jnp.where(rows + r * 256 < COLS, ref[rs, :], 0.0).astype(jnp.bfloat16)
+            return c
+        lax.fori_loop(0, CR // 256, one, 0)
+    pl.when(role_ref[0] == 0)(lambda: fill(h_ref))
+    pl.when(role_ref[0] != 0)(lambda: fill(a_ref))
+
+
+def head_cast(role, head, avg):
+    lanes = head.shape[1]
+    return pl.pallas_call(
+        cast_kernel,
+        grid_spec=pltpu.PrefetchScalarGridSpec(
+            num_scalar_prefetch=1, grid=(PADC // CR,),
+            in_specs=[pl.BlockSpec((CR, lanes), lambda j, r: (j * (1 - r[0]), 0)),
+                      pl.BlockSpec((CR, lanes), lambda j, r: (j * r[0], 0))],
+            out_specs=pl.BlockSpec((CR, lanes), lambda j, r: (j, 0))),
+        out_shape=jax.ShapeDtypeStruct((PADC, lanes), jnp.bfloat16),
+        compiler_params=pltpu.CompilerParams(vmem_limit_bytes=32 * 1024 * 1024),
+        name="head_cast",
+    )(role, head, avg)
+
+
+UR = 2048
+NB = -(-HALF // UR)
+LASTR = HALF - (NB - 1) * UR
+
+
+def games_of_block(k):
+    lo = [window_of(i) for i in range(GAMES // 2)]
+    return [i for i in range(GAMES // 2) if k * UR <= lo[i] < (k + 1) * UR]
+
+
+def update_kernel(role_ref, gall_ref, frow_ref, dlog_ref, h_hbm, m_hbm, a_hbm, ow, om, oa, oc, gr, dlt, buf, sems):
+    j = pl.program_id(0)
+    role = role_ref[0]
+    hbm = (h_hbm, m_hbm, a_hbm)
+
+    def copies(k, slot, rows, go):
+        for t in range(3):
+            c = pltpu.make_async_copy(hbm[t].at[pl.ds(pl.multiple_of(role * HALF + k * UR, 8), rows)],
+                                      buf.at[slot, t, pl.ds(0, rows)], sems.at[slot, t])
+            c.start() if go else c.wait()
+
+    def each(k, slot, go):
+        pl.when(k < NB - 1)(lambda: copies(k, slot, UR, go))
+        pl.when(k == NB - 1)(lambda: copies(k, slot, LASTR, go))
+
+    slot = lax.rem(j, 2)
+
+    @pl.when(j == 0)
+    def _():
+        each(j, slot, True)
+    each(j + 1, 1 - slot, True)
+
+    @pl.when(j == 0)
+    def _():
+        gr[...] = jnp.zeros_like(gr)
+        ids = gall_ref[...].reshape(-1, 128).astype(jnp.int32) - role * (GAMES // 2)
+        v = shift_rows(widen(dlog_ref[...]), ids_offset(ids), True)
+        for k in range(WIN // 128):
+            dlt[k * 128:(k + 1) * 128, :] = jnp.transpose(v[:, k * 128:(k + 1) * 128]).astype(jnp.bfloat16)
+    for k in range(NB):
+        todo = games_of_block(k)
+        if todo:
+            @pl.when(j == k)
+            def _(todo=todo):
+                own = gall_ref[...].reshape(-1, 128).astype(jnp.int32) - role * (GAMES // 2)
+                for i in todo:
+                    rhs = jnp.where(own == i, frow_ref[...].astype(jnp.float32), 0.0).astype(jnp.bfloat16)
+                    a = window_of(i)
+                    gr[a:a + WIN, :] = gr[a:a + WIN, :] + jnp.dot(dlt[...], rhs, preferred_element_type=jnp.float32)
+    each(j, slot, False)
+
+    def one(r, c):
+        rs = pl.ds(pl.multiple_of(r * 128, 128), 128)
+        g = gr[pl.ds(pl.multiple_of(j * UR + r * 128, 128), 128), :]
+        m = 0.5 * buf[slot, 1, rs, :] + g
+        w = buf[slot, 0, rs, :] - 4.0 * (g + 0.5 * m)
+        om[rs, :] = m
+        ow[rs, :] = w
+        oa[rs, :] = 0.5 * buf[slot, 2, rs, :] + 0.5 * w
+        oc[rs, :] = w.astype(jnp.bfloat16)
+        return c
+    lax.fori_loop(0, UR // 128, one, 0)
+
+
+def head_update(role, games_all, frow, dlog, head, moment, avg):
+    lanes = head.shape[1]
+    n = games_all.shape[0]
+    f32 = jnp.float32
+    S = jax.ShapeDtypeStruct
+    out = pl.BlockSpec((UR, lanes), lambda j, r: (j, 0))
+
+    def whole(*s):
+        return pl.BlockSpec(s, lambda j, r: (0,) * len(s))
+    hb = pl.BlockSpec(memory_space=pl.ANY)
+    return pl.pallas_call(
+        update_kernel,
+        grid_spec=pltpu.PrefetchScalarGridSpec(
+            num_scalar_prefetch=1, grid=(NB,),
+            in_specs=[whole(n, TB, 128), whole(n * TB, 128), whole(n, 16, 512), hb, hb, hb],
+            out_specs=(out,) * 4,
+            scratch_shapes=[pltpu.VMEM((NB * UR + WIN, lanes), f32), pltpu.VMEM((WIN, n * TB), jnp.bfloat16),
+                            pltpu.VMEM((2, 3, UR, lanes), f32), pltpu.SemaphoreType.DMA((2, 3))]),
+        out_shape=(S((HALF, lanes), f32),) * 3 + (S((HALF, lanes), jnp.bfloat16),),
+        compiler_params=pltpu.CompilerParams(vmem_limit_bytes=56 * 1024 * 1024),
+        name="head_update",
+    )(role, games_all, frow, dlog, head, moment, avg)
+
+
+def fast_device(
+    frames,
+    game_ids,
+    taken_actions,
+    next_actions,
+    expert_flags,
+    rewards,
+    done_flags,
+    weight_in,
+    weight_mid,
+    weight_out,
+    norm_gains,
+    head_table,
+    moment_in,
+    moment_mid,
+    moment_out,
+    moment_gains,
+    moment_head,
+    average_in,
+    average_mid,
+    average_out,
+    average_gains,
+    average_head,
+):
+    n = lax.axis_size("dp")
+    role_index = lax.axis_index("role")
+    online = role_index == 0
+    role = jnp.reshape(role_index, (1,)).astype(jnp.int32)
+    use_in = jnp.where(online, weight_in, average_in)[0].astype(jnp.bfloat16)
+    use_mid = jnp.where(online, weight_mid, average_mid)[0].astype(jnp.bfloat16)
+    use_out = jnp.where(online, weight_out, average_out)[0].astype(jnp.bfloat16)
+    use_gains = jnp.where(online, norm_gains, average_gains).astype(jnp.bfloat16)
+    gains3 = use_gains.astype(jnp.float32).reshape(-1, 128)
+
+    def lanes(v):
+        return jnp.broadcast_to(v.astype(jnp.float32)[:, None], (TB, 128))
+
+    ids = lanes(game_ids)
+    scal = jnp.stack(
+        [lanes(taken_actions), lanes(next_actions), lanes(expert_flags), lanes(rewards), lanes(done_flags), ids]
+    )
+    head_low = head_cast(role, head_table.T, average_head.T)
+    all_in, all_mid, all_out, all_gains, all_ids = gather([use_in, use_mid, use_out, gains3, ids], n, 1)
+    w_mid = all_mid.reshape(9 * MID, MID)
+    w_out = all_out.reshape(MID, D)
+    gains = all_gains.reshape(1, 4 * MID + 2 * D)
+    saved = forward(jnp.transpose(frames[0], (1, 0, 2)), all_in.reshape(D, MID), w_mid, w_out, gains)
+    dfeat, feat_rows, dlog, loss = head_stage(saved[-1], all_ids, scal, head_low, n, 2)
+    g_in, g_mid, g_out, g_gains = backward(dfeat, saved, w_mid, w_out, gains)
+    grad_out, grad_mid, grad_in, grad_gains = scatter(
+        [
+            g_out.reshape(n, MID // n, D),
+            g_mid.reshape(n, 9 * MID // n, MID),
+            g_in.reshape(n, D // n, MID),
+            g_gains.reshape(n, -1, 128),
+        ],
+        n,
+        3,
+    )
+    head_w, head_m, head_a, head_c = head_update(
+        role, all_ids, feat_rows, dlog, head_table.T, moment_head.T, average_head.T
+    )
+
+    def own(v):
+        return own_half(v, role_index)
+
+    in_w, in_m, in_a, in_c = renew(own(weight_in), grad_in[None], own(moment_in), own(average_in), learn_rate)
+    mid_w, mid_m, mid_a, mid_c = renew(
+        own(weight_mid), grad_mid[None], own(moment_mid), own(average_mid), learn_rate
+    )
+    out_w, out_m, out_a, out_c = renew(
+        own(weight_out), grad_out[None], own(moment_out), own(average_out), learn_rate
+    )
+    gain_w, gain_m, gain_a, gain_c = renew(
+        norm_gains, grad_gains.reshape(norm_gains.shape), moment_gains, average_gains, gain_rate
+    )
+    return (
+        loss[0, 0],
+        in_w,
+        grad_in[None],
+        in_a,
+        in_c,
+        mid_w,
+        mid_m,
+        mid_a,
+        mid_c,
+        out_w,
+        out_m,
+        out_a,
+        out_c,
+        gain_w,
+        gain_m,
+        gain_a,
+        gain_c,
+        head_w.T,
+        head_m.T,
+        head_a.T,
+        head_c.T,
+    )
+
+
 def solution(mesh):
     return jax.shard_map(
-        on_device,
+        fast_device if mesh.shape["dp"] == 16 else on_device,
         mesh=mesh,
         in_specs=(
             P("role", "dp", None, None),

time: 842 us -> 407 us (0.48); the launches traced: 829 us -> 406 us
  Pallas kernels: 0 us -> 378 us
  local copies, waits for them, and re-layouts: 304 us -> 9.24 us
  blocking collectives: 145 us -> 0 us
  other arithmetic: 140 us -> 17.8 us
  waiting for transfers between devices: 112 us -> 0 us
  matrix products: 92 us -> 0 us
  between operations: 19.5 us -> 0.84 us
  starting transfers between devices: 16.6 us -> 0 us
    pallas_call x0 -> x7, Pallas kernels: none -> 378 us  [the longest x1 165 us: scatter(): pl.pallas_call(functools.partial(scatter_kernel, nz, na), out_shape=tuple...]
    dot_general x13 -> x0, matrix products: 92 us -> none  [the longest x1 14.7 us: block_backward(): jnp.einsum('bpm,km->bpk', d_two, w_mid, preferred_element_type=jnp.float32)]
    unnamed x163 -> x46, local copies, waits for them, and re-layouts: 93.7 us -> 4.78 us
    reduce_scatter x4 -> x0, waiting for transfers between devices: 86.2 us -> none  [the longest x3 59 us: on_device(): reduced = lax.psum_scatter(stacked, 'dp', scatter_dimension=1, tiled=True)]
    all_gather x3 -> x0, blocking collectives: 59.1 us -> none  [the longest x1 22.3 us: on_device(): lax.all_gather(use_gains[layer], 'dp', axis=0, tiled=True)]
    psum x2 -> x0, blocking collectives: 56.3 us -> none  [on_device(): total_counts, total_sums = lax.psum((counts, sums), 'dp')]
    reshape x5 -> x2, local copies, waits for them, and re-layouts: 57.7 us -> 2.03 us  [the longest x1 1.4 us: fast_device(): gains = all_gains.reshape(1, 4 * MID + 2 * D)]
    reduce_sum x24 -> x0, other arithmetic: 55.4 us -> none  [the longest x4 30.8 us: group_norm(): return normed * gain + shift]
  transfers between devices with their start and end apart: 16 -> 0, of which waited for: 6 -> 0; matrix products, arithmetic and copies ran while one was open for 39% -> 0% of each run, Pallas kernels for 0% -> 0%
where the time goes in v1:
time: 407 us; the launch traced here: 406 us
  Pallas kernels  378 us (93%)
  other arithmetic  17.8 us (4%)
  local copies, waits for them, and re-layouts  9.24 us (2%)
    pallas_call x1, Pallas kernels, scatter(): pl.pallas_call(functools.partial(scatter_kernel, nz, na), out_shape=tuple...  165 us
    pallas_call x1, Pallas kernels, gather(): pl.pallas_call(functools.partial(gather_kernel, nz, na), out_shape=tuple(...  54.5 us
    pallas_call x1, Pallas kernels, backward(): pl.pallas_call(bwd_kernel, out_shape=(S((D, MID), f32), S((9 * MID, MID),...  47.8 us
    pallas_call x1, Pallas kernels, head_stage(): pl.pallas_call(functools.partial(head_kernel, n), out_shape=(S((TB, D), f...  41.8 us
    pallas_call x1, Pallas kernels, forward(): pl.pallas_call(fwd_kernel, out_shape=(S((ROWS, D), b16), S((ROWS, MID), f...  34.4 us
    pallas_call x1, Pallas kernels, head_update(): pl.pallas_call(update_kernel, grid_spec=pltpu.PrefetchScalarGridSpec(num_...  24.2 us
    pallas_call x1, Pallas kernels, head_cast(): pl.pallas_call(cast_kernel, grid_spec=pltpu.PrefetchScalarGridSpec(num_sc...  10.6 us

profile of v1, /device:TPU:6, one launch (start us, length us, event | category | flops | bytes accessed | tf_op | source)
XLA Modules:
  0.0 406.1 jit_solution(11436582810046498965)
XLA Ops:
  0.7 1.7 fusion.3.refs_0_
  2.3 1.9 fusion.refs_1_
  4.2 1.6 fusion.4.refs_2_
  5.8 1.3 fusion.9
  7.7 0.7 broadcast_in_dim.8.refs_4_
  8.4 54.5 %weights_gather.1 = (bf16[16,128,512]{2,1,0:T(8,128)(2,1)}, bf16[16,288,512]{2,1,0:T(8,128)(2,1)}, bf16[16,32,2048]{2,1,0:T(8,128)(2,1)}, f32[16,3,128]{2,1,0:T(4,128)}, f32[16,8,128]{2,1,0:T(8,128)}) custom-call(bf16[128,512]{1,0:T(8,128)(2,1)} %fusion.3.refs_0_, bf16[288,512]{1,0:T(8,128)(2,1)} %fusion.refs_1_, bf16[32,2048]{1,0:T(8,128)(2,1)} %fusion.4.refs_2_, ...), custom_call_target="tpu_custom_call" | custom-call | tf_op jit(solution)/shard_map/weights_gather/pallas_call | solution.py:784
  62.9 1.4 reshape.86.g_ref
  64.3 34.4 %block_forward.1 = (bf16[1056,2048]{1,0:T(8,128)(2,1)}, f32[1056,512]{1,0:T(8,128)}, f32[1056,512]{1,0:T(8,128)}, f32[1056,2048]{1,0:T(8,128)}, bf16[1056,512]{1...) custom-call(bf16[121,8,2048]{2,1,0:T(8,128)(2,1)} %bitcast.68, ...), custom_call_target="tpu_custom_call" | custom-call | tf_op jit(solution)/shard_map/block_forward/pallas_call | solution.py:529
  99.2 10.6 %head_cast.1.head_ref = bf16[36864,128]{1,0:T(8,128)(2,1)S(1)} custom-call(s32[1]{0:T(128)} %bitcast.8.role_ref, f32[36720,128]{1,0:T(8,128)} %bitcast.56, f32[36720,128]{1,0:T(8,128)} %bitcast.58), custom_call_target="tpu_custom_call" | custom-call | tf_op jit(solution)/shard_map/head_cast/pallas_call | solution.py:1188
  109.8 3.7 copy-done
  113.5 41.8 %head_stage.1 = (f32[8,2048]{1,0:T(8,128)}, bf16[128,128]{1,0:T(8,128)(2,1)}, bf16[16,16,512]{2,1,0:T(8,128)(2,1)}, f32[8,128]{1,0:T(8,128)}) custom-call(f32[8,2048]{1,0:T(8,128)} %get-tuple-element.54.feat_ref, f32[16,8,128]{2,1,0:T(8,128)} %get-tuple-element.55.gall_ref, f32[6,8,128]{2,1,0:T(8,128)} %copy-done.10, bf16[36864,128]{1,0:T(8,128)(2,1)} %copy-done), custom_call_target="tpu_custom_call" | custom-call | tf_op jit(solution)/shard_map/head_stage/pallas_call | solution.py:1154
  155.3 1.2 slice.3
  156.5 47.8 %block_backward.1 = (f32[2048,512]{1,0:T(8,128)}, f32[4608,512]{1,0:T(8,128)}, f32[512,2048]{1,0:T(8,128)}, f32[1,6144]{1,0:T(1,128)}) custom-call(f32[8,2048]{1,0:T(8,128)} %get-tuple-element.57.dfeat_ref, bf16[1056,2048]{1,0:T(8,128)(2,1)} %get-tuple-element.58.x_ref, f32[1056,512]{1,0:T(8,128)} %get-tuple-element.59.h1_ref, ...), custom_call_target="tpu_custom_call" | custom-call | tf_op jit(solution)/shard_map/block_backward/pallas_call | solution.py:661
  204.8 1.4 reduce.5
  207.0 164.9 %gradient_sums.1 = (f32[32,1024]{1,0:T(8,128)}, f32[288,256]{1,0:T(8,128)}, f32[128,256]{1,0:T(8,128)}, f32[3,128]{1,0:T(4,128)}) custom-call(f32[16,32,2048]{2,1,0:T(8,128)} %bitcast.67, f32[16,288,512]{2,1,0:T(8,128)} %bitcast.63, f32[16,128,512]{2,1,0:T(8,128)} %bitcast.66, f32[16,3,128]{2,1,0:T(4,128)} %reshape.91.refs_3_), custom_call_target="tpu_custom_call" | custom-call | tf_op jit(solution)/shard_map/gradient_sums/pallas_call | solution.py:914
  371.9 1.7 fusion.18
  373.6 0.7 add_multiply_fusion.2
  374.3 1.9 fusion.16
  376.2 0.8 add_multiply_fusion
  377.0 1.7 fusion.14
  378.6 0.7 add_multiply_fusion.1
  379.3 1.3 fusion.12
  381.2 24.2 %head_update.1 = (f32[18360,128]{1,0:T(8,128)}, f32[18360,128]{1,0:T(8,128)}, f32[18360,128]{1,0:T(8,128)}, bf16[18360,128]{1,0:T(8,128)(2,1)}) custom-call(s32[1]{0:T(128)} %bitcast.8.role_ref, f32[16,8,128]{2,1,0:T(8,128)} %get-tuple-element.55.gall_ref, bf16[128,128]{1,0:T(8,128)(2,1)} %get-tuple-element.73.frow_ref, ...), custom_call_target="tpu_custom_call" | custom-call | tf_op jit(solution)/shard_map/head_update/pallas_call | solution.py:1275
  405.4 0.7 copy.54
  (53 shorter events, 2.9 us)
Async XLA Ops:
  64.3 34.5 %copy-start.16 = (s32[8]{0:T(128)S(1)}, s32[8]{0:T(128)}, u32[]{:S(2)}) copy-start(s32[8]{0:T(128)} %param.24) | copy-start | bytes 100
  64.3 34.5 %copy-start.17 = (s32[8]{0:T(128)S(1)}, s32[8]{0:T(128)}, u32[]{:S(2)}) copy-start(s32[8]{0:T(128)} %param.25) | copy-start | bytes 100
  64.3 34.6 %copy-start.18 = (s32[8]{0:T(128)S(1)}, s32[8]{0:T(128)}, u32[]{:S(2)}) copy-start(s32[8]{0:T(128)} %param.26) | copy-start | bytes 100
  64.3 34.7 %copy-start.15 = (f32[8]{0:T(128)S(1)}, f32[8]{0:T(128)}, u32[]{:S(2)}) copy-start(f32[8]{0:T(128)} %param.27) | copy-start | bytes 100
  64.3 34.8 %copy-start.19 = (s32[8]{0:T(128)S(1)}, s32[8]{0:T(128)}, u32[]{:S(2)}) copy-start(s32[8]{0:T(128)} %param.28) | copy-start | bytes 100
  99.2 10.6 %copy-start.10 = (f32[6,8,128]{2,1,0:T(8,128)}, f32[6,8,128]{2,1,0:T(8,128)S(1)}, u32[]{:S(2)}) copy-start(f32[6,8,128]{2,1,0:T(8,128)S(1)} %constant_dynamic-update-slice_fusion.scal_ref) | copy-start | bytes 73732
  109.8 3.7 copy-start
  206.9 166.7 %copy-start.5 = (f32[1,128,512]{2,1,0:T(8,128)S(1)}, f32[1,128,512]{2,1,0:T(8,128)}, u32[]{:S(2)}) copy-start(f32[1,128,512]{2,1,0:T(8,128)} %param.39) | copy-start | bytes 786436
  206.9 167.4 %copy-start.2 = (f32[1,288,512]{2,1,0:T(8,128)S(1)}, f32[1,288,512]{2,1,0:T(8,128)}, u32[]{:S(2)}) copy-start(f32[1,288,512]{2,1,0:T(8,128)} %param.30) | copy-start | bytes 1769476
  206.9 169.3 %copy-start.1 = (f32[1,288,512]{2,1,0:T(8,128)S(1)}, f32[1,288,512]{2,1,0:T(8,128)}, u32[]{:S(2)}) copy-start(f32[1,288,512]{2,1,0:T(8,128)} %param.40) | copy-start | bytes 1769476
  206.9 170.1 %copy-start.4 = (f32[1,32,2048]{2,1,0:T(8,128)S(1)}, f32[1,32,2048]{2,1,0:T(8,128)}, u32[]{:S(2)}) copy-start(f32[1,32,2048]{2,1,0:T(8,128)} %param.31) | copy-start | bytes 786436
  206.9 171.7 %copy-start.6 = (f32[1,32,2048]{2,1,0:T(8,128)S(1)}, f32[1,32,2048]{2,1,0:T(8,128)}, u32[]{:S(2)}) copy-start(f32[1,32,2048]{2,1,0:T(8,128)} %param.41) | copy-start | bytes 786436
  206.9 172.4 %copy-start.11 = (f32[1,384]{1,0:T(1,128)S(1)}, f32[1,384]{1,0:T(1,128)}, u32[]{:S(2)}) copy-start(f32[1,384]{1,0:T(1,128)} %param.32) | copy-start | bytes 4612
  206.9 172.4 %copy-start.14 = (f32[1,384]{1,0:T(1,128)S(1)}, f32[1,384]{1,0:T(1,128)}, u32[]{:S(2)}) copy-start(f32[1,384]{1,0:T(1,128)} %param.37) | copy-start | bytes 4612
  206.9 173.7 %copy-start.13 = (f32[1,384]{1,0:T(1,128)S(1)}, f32[1,384]{1,0:T(1,128)}, u32[]{:S(2)}) copy-start(f32[1,384]{1,0:T(1,128)} %param.42) | copy-start | bytes 4612
  373.6 31.8 %copy-start.8 = (f32[1,128,256]{2,1,0:T(8,128)}, f32[1,128,256]{2,1,0:T(8,128)S(1)}, u32[]{:S(2)}) copy-start(f32[1,128,256]{2,1,0:T(8,128)S(1)} %get-tuple-element.112) | copy-start | bytes 393220
  376.2 29.2 %copy-start.3 = (f32[1,288,256]{2,1,0:T(8,128)}, f32[1,288,256]{2,1,0:T(8,128)S(1)}, u32[]{:S(2)}) copy-start(f32[1,288,256]{2,1,0:T(8,128)S(1)} %get-tuple-element.116) | copy-start | bytes 884740
  378.6 26.8 %copy-start.7 = (f32[1,32,1024]{2,1,0:T(8,128)}, f32[1,32,1024]{2,1,0:T(8,128)S(1)}, u32[]{:S(2)}) copy-start(f32[1,32,1024]{2,1,0:T(8,128)S(1)} %get-tuple-element.120) | copy-start | bytes 393220
  380.6 24.8 %copy-start.12 = (f32[1,384]{1,0:T(1,128)}, f32[1,384]{1,0:T(1,128)S(1)}, u32[]{:S(2)}) copy-start(f32[1,384]{1,0:T(1,128)S(1)} %get-tuple-element.124) | copy-start | bytes 4612
  381.2 24.3 %copy-start.9 = (f32[128,256]{1,0:T(8,128)S(1)}, f32[128,256]{1,0:T(8,128)}, u32[]{:S(2)}) copy-start(f32[128,256]{1,0:T(8,128)} %get-tuple-element.69) | copy-start | bytes 393220
